TPU v7x, 128 devices: a whole 4x4x4 slice. The times are simulated.
128 devices in a mesh: side: 2 (over core), dev: 64 (over z, y, x).
Axes of the slice: x: 4, y: 4, z: 4, core: 2. Of those that a mesh axis runs over, the one named last changes fastest.
Arguments:
- tokens: bfloat16 [512, 7168], P(('side', 'dev')), may hold values from -6 to 6
- routes: int32 [512, 8], P(('side', 'dev')), may hold values from 0 to 15, all different within a row; in each aligned block of 4 rows (0 to 3, 4 to 7, ...) at most 3 rows name the same one
- gates: float32 [512, 8], P(('side', 'dev')), may hold values from 0.05 to 0.6
- w_gate: bfloat16 [128, 7168, 256], P(('side', 'dev')), may hold values from -0.0625 to 0.0625
- w_up: bfloat16 [128, 7168, 256], P(('side', 'dev')), may hold values from -0.0625 to 0.0625
- w_down: bfloat16 [128, 256, 7168], P(('side', 'dev')), may hold values from -0.125 to 0.125
- queries: bfloat16 [512, 128, 576], P(('side', 'dev')), may hold values from -30 to 30
- cache: bfloat16 [512, 1024, 576], P(('side', 'dev')), may hold values from -5 to 5
- lengths: int32 [512], P(('side', 'dev')), may hold values from 2 to 1024, as said below
Outputs:
- moe_out: bfloat16 [512, 7168], P(('side', 'dev'))
- attention_out: bfloat16 [512, 128, 512], P(('side', 'dev'))
Inputs may be any that keep to these rules, and one draw needn't show every extreme that they name: `routes`: within each aligned block of 4 tokens (the rows of one device) no expert is named by more than 3 rows, a bound that some block reaches. `lengths`: some request has exactly 1024 valid positions.
All inputs are finite; a program needn't handle non-finite values.
Results may differ from a plain program's by a relative error of at most 0.0057.
Values may be sent and summed in bfloat16 or wider, within the bound.
A program may use at most 128 MiB of HBM per device.

v0:
```python
import jax
import jax.numpy as jnp
from jax import lax
from jax.sharding import PartitionSpec as P

LATENT = 512
ROPE = 64
NOPE = 128
TOP = 8
EXPERTS = 16
CAP = 3


def expert_rows(received, w_gate, w_up, w_down):
    width = received.shape[-1]
    rows = received.reshape(-1, width)
    gate = jnp.dot(rows, w_gate[0], preferred_element_type=jnp.float32)
    upper = jnp.dot(rows, w_up[0], preferred_element_type=jnp.float32)
    hidden = (jax.nn.silu(gate) * upper).astype(jnp.bfloat16)
    partial_value = jnp.dot(hidden, w_down[0], preferred_element_type=jnp.float32).astype(
        jnp.bfloat16
    )
    return partial_value.reshape(received.shape[:-1] + (partial_value.shape[-1],))


def attend(queries, cache, lengths):
    scale = (NOPE + ROPE) ** (-0.5)
    scores = jnp.einsum("rhk,rlk->rhl", queries, cache, preferred_element_type=jnp.float32) * scale
    valid = jnp.arange(cache.shape[1], dtype=jnp.int32)[None, None, :] < lengths[:, None, None]
    scores = jnp.where(valid, scores, -1e30)
    highest = jnp.max(scores, -1, keepdims=True)
    weights = jnp.where(valid, jnp.exp(scores - highest), 0.0)
    probabilities = (weights / jnp.sum(weights, -1, keepdims=True)).astype(jnp.bfloat16)
    return jnp.einsum(
        "rhl,rlk->rhk", probabilities, cache[:, :, :LATENT], preferred_element_type=jnp.float32
    ).astype(jnp.bfloat16)


def per_device(tokens, routes, gates, w_gate, w_up, w_down, queries, cache, lengths):
    count = lax.axis_size("side") * lax.axis_size("dev")
    slices = count // EXPERTS
    local_rows = tokens.shape[0]
    width = tokens.shape[1]
    onehot = (routes[:, :, None] == jnp.arange(EXPERTS, dtype=jnp.int32)[None, None, :]).astype(
        jnp.int32
    )
    per_token = jnp.sum(onehot, 1)
    before = jnp.cumsum(per_token, 0) - per_token
    slot = jnp.sum(onehot * before[:, None, :], 2)
    target = routes * CAP + slot
    placing = jnp.sum(
        (target[:, :, None] == jnp.arange(EXPERTS * CAP, dtype=jnp.int32)[None, None, :]).astype(
            jnp.bfloat16
        ),
        1,
    )
    packed = lax.dot_general(
        placing, tokens, (((0,), (0,)), ((), ())), preferred_element_type=jnp.float32
    ).astype(jnp.bfloat16)
    outgoing = jnp.broadcast_to(
        packed.reshape(EXPERTS, 1, CAP, width), (EXPERTS, slices, CAP, width)
    ).reshape(count, CAP, width)
    returned = lax.all_to_all(
        expert_rows(
            lax.all_to_all(outgoing, ("side", "dev"), split_axis=0, concat_axis=0, tiled=True),
            w_gate,
            w_up,
            w_down,
        ),
        ("side", "dev"),
        split_axis=0,
        concat_axis=0,
        tiled=True,
    )
    flat_back = returned.reshape(count * CAP, width)
    lookup = (
        routes[:, :, None] * slices + jnp.arange(slices, dtype=jnp.int32)[None, None, :]
    ) * CAP + slot[:, :, None]
    picked = (
        jnp.take(flat_back, lookup.reshape(-1), axis=0)
        .reshape(local_rows, TOP * slices, width)
        .astype(jnp.float32)
    )
    weights = jnp.repeat(gates, slices, axis=1)
    moe_out = jnp.sum(picked * weights[:, :, None], 1).astype(jnp.bfloat16)
    attention_out = attend(queries, cache, lengths)
    return (moe_out, attention_out)


def solution(mesh):
    in_specs = (
        P(("side", "dev"), None),
        P(("side", "dev"), None),
        P(("side", "dev"), None),
        P(("side", "dev"), None, None),
        P(("side", "dev"), None, None),
        P(("side", "dev"), None, None),
        P(("side", "dev"), None, None),
        P(("side", "dev"), None, None),
        P(("side", "dev")),
    )
    out_specs = (P(("side", "dev"), None), P(("side", "dev"), None, None))
    return jax.shard_map(
        per_device, mesh=mesh, in_specs=in_specs, out_specs=out_specs, check_vma=False
    )
```

profile of v0, /device:TPU:85, one launch (start us, length us, event | category | flops | bytes accessed | tf_op | source)
XLA Modules:
  0.0 284.8 jit_solution(18060879468319179731)
XLA Ops:
  0.6 0.0 copy-start
  0.6 0.8 convert_reduce_fusion
  1.5 0.9 select_reduce_fusion
  2.4 0.7 multiply_add_fusion.1
  3.1 0.1 fusion.23
  3.2 1.2 convolution_convert_fusion.1
  4.4 0.4 broadcast_in_dim.51
  4.9 5.2 %broadcast_in_dim.52 = bf16[16,8,3,7168]{3,2,1,0:T(4,128)(2,1)} broadcast(bf16[16,3,7168]{2,1,0:T(4,128)(2,1)S(1)} %broadcast_in_dim.51), dimensions={0,2,3} | broadcast | bytes 6193152 | tf_op jit(solution)/shard_map/broadcast_in_dim | solution.py:60
  10.1 96.1 %all_to_all.10 = bf16[128,3,7168]{2,1,0:T(4,128)(2,1)} all-to-all(bf16[128,3,7168]{2,1,0:T(4,128)(2,1)} %bitcast.24), channel_id=1, replica_groups=mesh['side'=2,'dev'=64] {'side','dev'}, dimensions={0} | all-to-all | bytes 11010048 | tf_op jit(solution)/shard_map/all_to_all | solution.py:65
  106.2 13.0 %reshape.127 = bf16[384,7168]{1,0:T(8,128)(2,1)} reshape(bf16[128,3,7168]{2,1,0:T(4,128)(2,1)} %all_to_all.10) | data formatting | bytes 11010048 | tf_op jit(solution)/shard_map/reshape | solution.py:16
  119.3 5.4 %fusion.6 = f32[384,256]{1,0:T(8,128)S(1)} fusion(bf16[384,7168]{1,0:T(8,128)(2,1)} %reshape.127, bf16[1,7168,256]{2,1,0:T(8,128)(2,1)} %param.12), kind=kOutput, calls=%fused_computation.10 | convolution fusion | flops 1409286144 | bytes 9568256 | tf_op jit(solution)/shard_map/dot_general | solution.py:17
  124.7 0.9 copy-done.6
  125.6 1.6 fusion.15
  127.2 0.4 copy-done.3
  127.6 4.0 %convolution_convert_fusion = bf16[384,7168]{1,0:T(8,128)(2,1)} fusion(bf16[384,256]{1,0:T(8,128)(2,1)S(1)} %fusion.15, bf16[1,256,7168]{2,1,0:T(8,128)(2,1)S(1)} %copy-done.3), kind=kOutput, calls=%fused_computation.2 | convolution fusion | flops 1412038656 | bytes 9371648 | tf_op jit(solution)/shard_map/dot_general | solution.py:20
  131.6 12.3 %reshape.128 = bf16[128,3,7168]{2,1,0:T(4,128)(2,1)} reshape(bf16[384,7168]{1,0:T(8,128)(2,1)} %convolution_convert_fusion) | data formatting | bytes 11010048 | tf_op jit(solution)/shard_map/reshape | solution.py:23
  143.9 11.5 %all-to-all-start.1 = ((bf16[128,3,7168]{2,1,0:T(4,128)(2,1)}), bf16[128,3,7168]{2,1,0:T(4,128)(2,1)}, u32[]{:S(2)}, u32[]{:S(2)}) async-start(bf16[128,3,7168]{2,1,0:T(4,128)(2,1)} %reshape.128), calls=%async_computation.1 | async-start | bytes 14680064 | tf_op jit(solution)/shard_map/all_to_all | solution.py:63
  155.4 0.1 multiply_add_fusion
  155.5 0.1 add.90
  155.6 0.1 add.85
  155.7 0.1 broadcast_in_dim.54
  155.7 0.1 mul.73
  155.9 0.0 copy-done.5
  155.9 0.1 iota_compare_fusion
  155.9 0.0 copy-done
  155.9 4.0 %fusion.26 = (f32[4,128]{1,0:T(4,128)S(1)}, f32[4,128,1024]{2,1,0:T(8,128)S(1)}) fusion(pred[4,1024]{1,0:T(4,128)(4,1)S(1)} %iota_compare_fusion, bf16[4,128,576]{1,2,0:T(8,128)(2,1)S(1)} %copy-done, bf16[4,1024,576]{1,2,0:T(8,128)(2,1)} %param.16), kind=kOutput, calls=%fused_computation.39 | convolution fusion | flops 606602240 | bytes 7411712 | tf_op jit(solution)/shard_map/sub | solution.py:32
  159.9 4.5 %fusion.9 = bf16[4,128,512]{2,1,0:T(8,128)(2,1)} fusion(bf16[4,1024,576]{1,2,0:T(8,128)(2,1)} %param.16, f32[4,128,1024]{2,1,0:T(8,128)S(1)} %get-tuple-element.5, f32[4,128]{1,0:T(4,128)S(1)} %get-tuple-element.4), kind=kOutput, calls=%fused_computation.16 | convolution fusion | flops 538181632 | bytes 6817792 | tf_op jit(solution)/shard_map/rhl,rlk->rhk/dot_general | solution.py:34
  164.5 91.8 %all-to-all-done.1 = bf16[128,3,7168]{2,1,0:T(4,128)(2,1)} async-done(((bf16[128,3,7168]{2,1,0:T(4,128)(2,1)}), bf16[128,3,7168]{2,1,0:T(4,128)(2,1)}, u32[]{:S(2)}, u32[]{:S(2)}) %all-to-all-start.1) | async-done | bytes 5505056 | tf_op jit(solution)/shard_map/all_to_all | solution.py:63
  256.3 13.0 %reshape.129 = bf16[384,7168]{1,0:T(8,128)(2,1)} reshape(bf16[128,3,7168]{2,1,0:T(4,128)(2,1)} %all-to-all-done.1) | data formatting | bytes 11010048 | tf_op jit(solution)/shard_map/reshape | solution.py:75
  269.3 11.3 %gather_fusion = bf16[256,7168]{1,0:T(8,128)(2,1)} fusion(bf16[384,7168]{1,0:T(8,128)(2,1)} %reshape.129, s32[1024]{0:T(1024)S(1)} %pad_clamp_fusion), kind=kCustom, calls=%fused_computation | custom fusion | bytes 7341056 | tf_op jit(solution)/shard_map/jit(_take)/gather | solution.py:80
  280.6 4.1 %multiply_reduce_fusion = bf16[4,7168]{1,0:T(4,128)(2,1)} fusion(f32[4,64]{1,0:T(4,128)S(1)} %mul.73, pred[4,64]{1,0:T(4,128)(4,1)S(1)} %compare_and_fusion, bf16[256,7168]{1,0:T(8,128)(2,1)} %gather_fusion), kind=kLoop, calls=%fused_computation.4 | loop fusion | flops 7311360 | bytes 3728640 | tf_op jit(solution)/shard_map/reduce_sum | solution.py:85
  284.7 0.0 copy-done.1
  (13 shorter events, 0.1 us)
Async XLA Ops:
  0.6 155.3 %copy-start = (bf16[4,128,576]{1,2,0:T(8,128)(2,1)S(1)}, bf16[4,128,576]{1,2,0:T(8,128)(2,1)}, u32[]{:S(2)}) copy-start(bf16[4,128,576]{1,2,0:T(8,128)(2,1)} %param.15) | copy-start | bytes 1769476
  119.3 5.4 %copy-start.2 = (bf16[384,7168]{1,0:T(8,128)(2,1)S(1)}, bf16[384,7168]{1,0:T(8,128)(2,1)}, u32[]{:S(2)}) copy-start(bf16[384,7168]{1,0:T(8,128)(2,1)} %reshape.127) | copy-start | bytes 16515076
  119.3 6.3 %copy-start.6 = (bf16[1,7168,256]{2,1,0:T(8,128)(2,1)S(1)}, bf16[1,7168,256]{2,1,0:T(8,128)(2,1)}, u32[]{:S(2)}) copy-start(bf16[1,7168,256]{2,1,0:T(8,128)(2,1)} %param.13) | copy-start | bytes 11010052
  125.6 2.0 copy-start.3
  143.9 11.7 %copy-start.4 = (f32[4,8]{1,0:T(4,128)S(1)}, f32[4,8]{1,0:T(4,128)}, u32[]{:S(2)}) copy-start(f32[4,8]{1,0:T(4,128)} %param.11) | copy-start | bytes 388
  143.9 11.9 %copy-start.5 = (s32[4]{0:T(128)S(1)}, s32[4]{0:T(128)}, u32[]{:S(2)}) copy-start(s32[4]{0:T(128)} %param.17) | copy-start | bytes 52
  143.9 112.3 %all-to-all-start.1 = ((bf16[128,3,7168]{2,1,0:T(4,128)(2,1)}), bf16[128,3,7168]{2,1,0:T(4,128)(2,1)}, u32[]{:S(2)}, u32[]{:S(2)}) async-start(bf16[128,3,7168]{2,1,0:T(4,128)(2,1)} %reshape.128), calls=%async_computation.1 | async-start | bytes 14680064 | tf_op jit(solution)/shard_map/all_to_all | solution.py:63
  269.3 15.5 %copy-start.1 = (bf16[4,128,576]{1,2,0:T(8,128)(2,1)S(1)}, bf16[4,128,576]{1,2,0:T(8,128)(2,1)}, u32[]{:S(2)}) copy-start(bf16[4,128,576]{1,2,0:T(8,128)(2,1)} %param.15) | copy-start | bytes 1769476
where the time goes:
time: 286 us; the launch traced here: 285 us
  blocking collectives  96.1 us (34%)
  waiting for transfers between devices  91.8 us (32%)
  local copies, waits for them, and re-layouts  57.1 us (20%)
  matrix products  20.7 us (7%)
  starting transfers between devices  11.5 us (4%)
  other arithmetic  6.84 us (2%)
    all_to_all x1, blocking collectives, per_device(): lax.all_to_all(outgoing, ('side', 'dev'), split_axis=0, concat_axis=0, ti...  96.1 us
    all_to_all x1, waiting for transfers between devices, per_device(): lax.all_to_all(expert_rows(lax.all_to_all(outgoing, ('side', 'dev'), spli...  91.8 us
    reshape x1, local copies, waits for them, and re-layouts, expert_rows(): rows = received.reshape(-1, width)  13 us
    reshape x1, local copies, waits for them, and re-layouts, per_device(): flat_back = returned.reshape(count * CAP, width)  13 us
    reshape x1, local copies, waits for them, and re-layouts, expert_rows(): partial_value.reshape(received.shape[:-1] + (partial_value.shape[-1],))  12.3 us
    all_to_all x1, starting transfers between devices, per_device(): lax.all_to_all(expert_rows(lax.all_to_all(outgoing, ('side', 'dev'), spli...  11.5 us
    gather x1, local copies, waits for them, and re-layouts, per_device(): jnp.take(flat_back, lookup.reshape(-1), axis=0)  11.3 us
  transfers between devices with their start and end apart: 1, of which 1 were waited for; matrix products, arithmetic and copies ran while one was open for 3% of the time, Pallas kernels for 0%

commit v1 on v0

v1 whole, which is shorter than its diff:
```python
import jax
import jax.numpy as jnp
from jax import lax
from jax.sharding import PartitionSpec as P

LATENT = 512
ROPE = 64
NOPE = 128
EXPERTS = 16


def attend(queries, cache, lengths):
    scale = (NOPE + ROPE) ** (-0.5)
    scores = jnp.einsum("rhk,rlk->rhl", queries, cache, preferred_element_type=jnp.float32) * scale
    valid = jnp.arange(cache.shape[1], dtype=jnp.int32)[None, None, :] < lengths[:, None, None]
    scores = jnp.where(valid, scores, -1e30)
    highest = jnp.max(scores, -1, keepdims=True)
    weights = jnp.where(valid, jnp.exp(scores - highest), 0.0)
    probabilities = (weights / jnp.sum(weights, -1, keepdims=True)).astype(jnp.bfloat16)
    return jnp.einsum(
        "rhl,rlk->rhk", probabilities, cache[:, :, :LATENT], preferred_element_type=jnp.float32
    ).astype(jnp.bfloat16)


def per_device(tokens, routes, gates, w_gate, w_up, w_down, queries, cache, lengths):
    axes = ("side", "dev")
    count = lax.axis_size("side") * lax.axis_size("dev")
    slices = count // EXPERTS
    me = lax.axis_index("side") * lax.axis_size("dev") + lax.axis_index("dev")
    expert = me // slices
    dense = jnp.sum(
        jnp.where(
            routes[:, :, None] == jnp.arange(EXPERTS, dtype=jnp.int32)[None, None, :],
            gates[:, :, None],
            0.0,
        ),
        1,
    )
    rows = lax.all_gather(tokens, axes, axis=0, tiled=True)
    weight = lax.all_gather(dense, axes, axis=0, tiled=True)
    own = jnp.sum(jnp.where(jnp.arange(EXPERTS)[None, :] == expert, weight, 0.0), 1)
    gate = jnp.dot(rows, w_gate[0], preferred_element_type=jnp.float32)
    upper = jnp.dot(rows, w_up[0], preferred_element_type=jnp.float32)
    hidden = (jax.nn.silu(gate) * upper).astype(jnp.bfloat16)
    partial = jnp.dot(hidden, w_down[0], preferred_element_type=jnp.float32) * own[:, None]
    moe_out = lax.psum_scatter(
        partial.astype(jnp.bfloat16), axes, scatter_dimension=0, tiled=True
    ).astype(jnp.bfloat16)
    attention_out = attend(queries, cache, lengths)
    return (moe_out, attention_out)


def solution(mesh):
    a = ("side", "dev")
    in_specs = (P(a, None),) * 3 + (P(a, None, None),) * 5 + (P(a),)
    out_specs = (P(a, None), P(a, None, None))
    return jax.shard_map(
        per_device, mesh=mesh, in_specs=in_specs, out_specs=out_specs, check_vma=False
    )
```

time: 286 us -> 527 us (1.84)
  the two profiles are of different devices: /device:TPU:85 before, /device:TPU:0 now
where the time goes in v1:
time: 527 us; the launch traced here: 525 us
  blocking collectives  320 us (61%)
  waiting for transfers between devices  144 us (27%)
  matrix products  31.4 us (6%)
  local copies, waits for them, and re-layouts  14.3 us (3%)
  between operations  14.1 us (3%)
    all_gather x1, blocking collectives, per_device(): weight = lax.all_gather(dense, axes, axis=0, tiled=True)  320 us
    unnamed x3, waiting for transfers between devices  144 us
    dot_general x1, matrix products, per_device(): jnp.dot(hidden, w_down[0], preferred_element_type=jnp.float32)  16 us
    unnamed x6, local copies, waits for them, and re-layouts  14.3 us
  transfers between devices with their start and end apart: 2, of which 1 were waited for; matrix products, arithmetic and copies ran while one was open for 2% of the time, Pallas kernels for 0%

profile of v1, /device:TPU:0, one launch (start us, length us, event | category | flops | bytes accessed | tf_op | source)
XLA Modules:
  0.0 525.4 jit_solution(9919417915235600856)
XLA Ops:
  7.2 0.0 copy-start
  7.2 0.0 all-gather.4.cloned.1.call-start
  7.2 0.7 all-gather.4.cloned.1.call-update
  7.9 0.0 all-reduce.3.cloned.1.call-start
  8.0 0.8 select_reduce_fusion.1
  8.8 320.2 %all-gather.1 = f32[128,4,16]{2,1,0:T(4,128)S(1)} all-gather(f32[1,4,16]{2,1,0:T(4,128)S(1)} %bitcast.24), channel_id=1, replica_groups=mesh['side'=2,'dev'=64] {'side','dev'}, dimensions={0}, use_global_device_ids=true | all-gather | bytes 33024 | tf_op jit(solution)/shard_map/all_gather | solution.py:40
  328.9 0.1 select_reduce_fusion
  329.1 0.0 all-gather.4.cloned.1.call-done
  329.1 12.1 %reshape.36 = bf16[512,7168]{1,0:T(8,128)(2,1)} reshape(bf16[128,4,7168]{2,1,0:T(4,128)(2,1)} %all-gather.4.cloned.1.call-done) | data formatting | bytes 14680064
  341.2 6.2 %fusion.6 = f32[512,256]{1,0:T(8,128)S(1)} fusion(bf16[512,7168]{1,0:T(8,128)(2,1)} %reshape.36, bf16[1,7168,256]{2,1,0:T(8,128)(2,1)} %param.12), kind=kOutput, calls=%fused_computation.7 | convolution fusion | flops 1879048192 | bytes 11534336 | tf_op jit(solution)/shard_map/dot_general | solution.py:42
  347.4 16.0 %multiply_convert_fusion = bf16[512,7168]{1,0:T(8,128)(2,1)} fusion(f32[512]{0:T(512)S(1)} %select_reduce_fusion, bf16[1,256,7168]{2,1,0:T(8,128)(2,1)} %param.14, bf16[512,7168]{1,0:T(8,128)(2,1)} %reshape.36, bf16[1,7168,256]{2,1,0:T(8,128)(2,1)} %param.13, f32[512,256]{1,0:T(8,128)S(1)} %fusion.6), kind=kOutput, calls=%fused_computation.1 | convolution fusion | flops 3766222848 | bytes 22546432 | tf_op jit(solution)/shard_map/dot_general | solution.py:45
  363.4 0.0 copy-start.1
  363.4 0.0 all-reduce.3.cloned.1.call-update
  363.4 0.6 copy-done.1
  364.1 0.1 iota_compare_fusion
  364.1 0.0 copy-done
  364.2 4.6 fusion.28
  368.8 4.6 fusion.9
  373.4 143.6 %all-reduce.3.cloned.1.call-done = bf16[512,7168]{1,0:T(8,128)(2,1)} async-done(((bf16[512,7168]{1,0:T(8,128)(2,1)}), bf16[512,7168]{1,0:T(8,128)(2,1)}) %all-reduce.3.cloned.1.call-update) | async-done | bytes 7340048
  517.0 1.6 constant_dynamic-slice_fusion
  (1 shorter events, 0.0 us)
Async XLA Ops:
  7.2 357.0 %copy-start = (bf16[4,128,576]{1,2,0:T(8,128)(2,1)S(1)}, bf16[4,128,576]{1,2,0:T(8,128)(2,1)}, u32[]{:S(2)}) copy-start(bf16[4,128,576]{1,2,0:T(8,128)(2,1)} %param.15) | copy-start | bytes 1769476
  7.2 321.9 %all-gather.4.cloned.1.call-start = ((), (), s32[]{:S(2)}) async-start(), calls=%async_computation | async-start | bytes 7397376 | tf_op jit(solution)/shard_map/all_gather | solution.py:39
  7.9 509.1 %all-reduce.3.cloned.1.call-start = ((), (), s32[]{:S(2)}) async-start(), calls=%async_computation.1 | async-start | bytes 14680064
  363.4 0.7 copy-start.1
Sparse Core Ops, SparseCore 0:
  11.0 71.7 all-gather.3
  363.6 153.4 all-reduce.2

commit v2 on v1

v2 whole, which is shorter than its diff:
```python
import jax
import jax.numpy as jnp
from jax import lax
from jax.experimental import pallas as pl
from jax.experimental.pallas import tpu as pltpu
from jax.sharding import PartitionSpec as P

D = 7168
UNITS = 256
LATENT = 512
KEY = 576
HEADS = 128
MAX_LEN = 1024
REQ = 4
EXPERTS = 16
SCALE = 192.0 ** -0.5

QUARTER = 1792
PIECES = 3
WIDTH = 640
USED = (640, 640, 512)
ROWS = 16
BLOCKS = 64
STAGES = 6
SB_OFF = {5: 0, 4: 512, 3: 768, 2: 896, 1: 960, 0: 992}
MESH = pl.DeviceIdType.MESH
F32 = jnp.float32
BF16 = jnp.bfloat16


def beta_of(p, k, s):
    return s if ((k + p) // 3) % 2 == 0 else 1 - s


def bit_of(c, beta):
    if isinstance(c, int):
        high, low = c // 2, ((c + 1) // 2) % 2
    else:
        high, low = lax.div(c, 2), lax.rem(lax.div(c + 1, 2), 2)
    return beta * high + (1 - beta) * low


def flip_of(c, beta):
    return beta * (3 - c) + (1 - beta) * (c + 1 - 2 * lax.rem(c, 2))


def axis_part(p, s, a, c):
    k = (a - p) % 3
    return bit_of(c, beta_of(p, k, s)) * (1 << k) + bit_of(c, beta_of(p, k + 3, s)) * (1 << (k + 3))


def block_of(p, s, x, y, z):
    return axis_part(p, s, 0, x) + axis_part(p, s, 1, y) + axis_part(p, s, 2, z)


def start_of(n, k):
    return lax.div(n, 1 << k) * (1 << k)


def other_of(n, k):
    return n + (1 << k) * (1 - 2 * lax.rem(lax.div(n, 1 << k), 2))


def rows_of(n, count):
    return pl.ds(pl.multiple_of(n * ROWS, ROWS), count * ROWS)


def gather_plan():
    plan = [(0, -1, 0, False, 0, 1)]
    for k in range(1, STAGES):
        size = 1 << (k - 1)
        parts = 2 if k == 5 else 1
        for new in (False, True):
            for part in range(parts):
                plan.append((k, k - 1 if new else k - 2, k - 1, new, part * (size // parts), size // parts))
    return plan


PLAN = gather_plan()


def plan_region(n, entry):
    k, _, level, new, offset, size = entry
    base = start_of(other_of(n, level), level) if new else start_of(n, level)
    return base + offset, size


def kernel(
    tokens, routes, gates, lengths, w_gate, w_up, w_down, queries, cache,
    moe_out, att_out,
    x_buf, wg, wu, wd, kv, qs, att, acc, hid, gexp, total, sib_out, sib_in, out_buf, in_buf,
    pack, got, pack2, got2,
    local_sem, att_sem, a2a_send, a2a_recv, ag_send, ag_recv, sib_send, sib_recv,
    rsib_send, rsib_recv, rs_send, rs_recv, b2b_send, b2b_recv,
):
    s = lax.axis_index("side")
    dev = lax.axis_index("dev")
    x, y, z = lax.rem(dev, 4), lax.rem(lax.div(dev, 4), 4), lax.div(dev, 16)
    coords = (x, y, z)
    t = 1 - s

    def chip(cx, cy, cz):
        return cz * 16 + cy * 4 + cx

    def partner(p, k):
        a = (k + p) % 3
        new = list(coords)
        new[a] = flip_of(coords[a], beta_of(p, k, s))
        return (s, chip(*new))

    peers = [(s, chip(lax.rem(x + d, 4), y, z)) for d in (1, 2, 3)]
    sibling = (t, dev)

    loads = [
        pltpu.make_async_copy(queries, qs, local_sem.at[0]),
        pltpu.make_async_copy(cache, kv, local_sem.at[1]),
        pltpu.make_async_copy(w_gate.at[0], wg, local_sem.at[2]),
        pltpu.make_async_copy(w_up.at[0], wu, local_sem.at[3]),
        pltpu.make_async_copy(w_down.at[0], wd, local_sem.at[4]),
    ]

    barrier = pltpu.get_barrier_semaphore()
    greet = peers + [sibling] + [
        (s, chip(x, lax.rem(y + 1, 4), z)), (s, chip(x, lax.rem(y + 3, 4), z)),
        (s, chip(x, y, lax.rem(z + 1, 4))), (s, chip(x, y, lax.rem(z + 3, 4))),
    ]
    for who in greet:
        pl.semaphore_signal(barrier, inc=1, device_id=who, device_id_type=MESH)
    for load in loads:
        load.start()

    lane = lax.broadcasted_iota(jnp.int32, (4, 128), 1)
    dense = jnp.zeros((4, 128), F32)
    for k in range(8):
        dense += jnp.where(routes[:, k:k + 1] == (lane & 15), gates[:, k:k + 1], 0.0)
    first = dense.astype(BF16).astype(F32)
    second = (dense - first).astype(BF16).astype(F32)
    third = dense - first - second
    aux = jnp.where(lane < 16, first, jnp.where(lane < 32, second, jnp.where(lane < 48, third, 0.0)))
    aux = jnp.concatenate([aux, jnp.zeros((4, 128), F32)], 1)
    for j in range(4):
        parts = []
        for c in range(4):
            lo = QUARTER * j + 512 * c
            if c < 3:
                parts.append(tokens[:, lo:lo + 512].astype(F32))
            else:
                parts.append(jnp.concatenate([tokens[:, lo:lo + 256].astype(F32), aux], 1))
        pack[j] = jnp.concatenate(parts, 0).astype(BF16)

    pl.semaphore_wait(barrier, len(greet))

    def a2a(src, dst, send, recv):
        copies = []
        for i, who in enumerate(peers):
            to = lax.rem(x + i + 1, 4)
            copies.append(pltpu.make_async_remote_copy(
                src_ref=src.at[to], dst_ref=dst.at[x], send_sem=send.at[i], recv_sem=recv.at[i],
                device_id=who, device_id_type=MESH))
        for copy in copies:
            copy.start()
        dst[x] = src[x]
        return copies

    opened = a2a(pack, got, a2a_send, a2a_recv)
    for copy in opened:
        copy.wait()
    rows = got[...].reshape(64, 512)
    row = lax.broadcasted_iota(jnp.int32, (16, 64), 0)
    col = lax.broadcasted_iota(jnp.int32, (16, 64), 1)
    assembled = []
    for c in range(4):
        select = jnp.where(col == (row >> 2) * 16 + c * 4 + (row & 3), 1.0, 0.0).astype(BF16)
        assembled.append(jnp.dot(select, rows, preferred_element_type=F32).astype(BF16))
    assembled = jnp.concatenate(assembled, 1)

    own = [block_of(p, s, x, y, z) for p in range(PIECES)]
    theirs = [block_of(p, t, x, y, z) for p in range(PIECES)]
    for p in range(PIECES):
        x_buf[s, p, rows_of(own[p], 1), :] = assembled[:, WIDTH * p:WIDTH * (p + 1)]

    def ag_copy(p, i):
        begin, size = plan_region(own[p], PLAN[i])
        region = x_buf.at[s, p, rows_of(begin, size), :]
        return pltpu.make_async_remote_copy(
            src_ref=region, dst_ref=region, send_sem=ag_send.at[p, i], recv_sem=ag_recv.at[p, i],
            device_id=partner(p, PLAN[i][0]), device_id_type=MESH)

    def ag_arrival(p, i):
        begin, size = plan_region(other_of(own[p], PLAN[i][0]), PLAN[i])
        region = x_buf.at[s, p, rows_of(begin, size), :]
        return pltpu.make_async_remote_copy(
            src_ref=region, dst_ref=region, send_sem=ag_send.at[p, i], recv_sem=ag_recv.at[p, i],
            device_id=partner(p, PLAN[i][0]), device_id_type=MESH), begin, size

    final = [i for i in range(len(PLAN)) if PLAN[i][0] == 5]

    def forward_region(p, n, f):
        if f == 0:
            return start_of(n, 3), 8
        if f == 1:
            return start_of(other_of(n, 3), 3), 8
        if f == 2:
            return start_of(other_of(n, 4), 4), 16
        return plan_region(other_of(n, 5), PLAN[final[f - 3]])

    def forward(p, f, n, side):
        begin, size = forward_region(p, n, f)
        region = x_buf.at[side, p, rows_of(begin, size), :]
        return pltpu.make_async_remote_copy(
            src_ref=region, dst_ref=region, send_sem=sib_send.at[p, f], recv_sem=sib_recv.at[p, f],
            device_id=sibling, device_id_type=MESH)

    def ag_start(trigger, p):
        for i, entry in enumerate(PLAN):
            if entry[1] == trigger:
                ag_copy(p, i).start()

    def attend(r):
        scores = lax.dot_general(
            qs[r], kv[r], (((1,), (1,)), ((), ())), preferred_element_type=F32) * SCALE
        valid = lax.broadcasted_iota(jnp.int32, (HEADS, MAX_LEN), 1) < lengths[r]
        scores = jnp.where(valid, scores, -1e30)
        highest = jnp.max(scores, -1, keepdims=True)
        weights = jnp.where(valid, jnp.exp(scores - highest), 0.0)
        chance = (weights / jnp.sum(weights, -1, keepdims=True)).astype(BF16)
        att[r] = jnp.dot(chance, kv[r, :, :LATENT], preferred_element_type=F32).astype(BF16)
        pltpu.make_async_copy(att.at[r], att_out.at[r], att_sem.at[r]).start()

    for p in range(PIECES):
        ag_start(-1, p)
    for k in range(5):
        for p in range(PIECES):
            for i, entry in enumerate(PLAN):
                if entry[0] == k:
                    ag_arrival(p, i)[0].wait_recv()
            ag_start(k, p)
        if k >= 2:
            for p in range(PIECES):
                forward(p, k - 2, own[p], s).start()
        if k == 3:
            loads[0].wait()
            loads[1].wait()
            attend(0)
            attend(1)
        if k == 4:
            attend(2)
            attend(3)
    for f, i in enumerate(final):
        for p in range(PIECES):
            ag_arrival(p, i)[0].wait_recv()
            forward(p, 3 + f, own[p], s).start()

    loads[2].wait()
    loads[3].wait()

    def project(side):
        for p in range(PIECES):
            w = USED[p]

            def step(q, carry):
                base = axis_part(p, side, 0, q)
                tiles = []
                for zz in range(4):
                    for yy in range(4):
                        n = base + axis_part(p, side, 1, yy) + axis_part(p, side, 2, zz)
                        tiles.append(x_buf[side, p, rows_of(n, 1), :w])
                lhs = jnp.concatenate(tiles, 0)
                deep = pl.ds(pl.multiple_of(q * QUARTER + p * WIDTH, 128), w)
                acc[side, :, :UNITS] += jnp.dot(lhs, wg[deep, :], preferred_element_type=F32)
                acc[side, :, UNITS:] += jnp.dot(lhs, wu[deep, :], preferred_element_type=F32)
                return carry

            lax.fori_loop(0, 4, step, 0)
        gate, upper = acc[side, :, :UNITS], acc[side, :, UNITS:]
        hid[side] = (gate / (1.0 + jnp.exp(-gate)) * upper).astype(BF16)
        expert = s * 8 + z * 2 + lax.div(y, 2)
        deep_lane = lax.broadcasted_iota(jnp.int32, (128, 128), 0)
        select = jnp.where(((deep_lane & 15) == expert) & (deep_lane < 48), 1.0, 0.0).astype(BF16)
        tiles = []
        for zz in range(4):
            for yy in range(4):
                n = axis_part(2, side, 1, yy) + axis_part(2, side, 2, zz)
                tiles.append(x_buf[side, 2, rows_of(n, 1), 512:640])
        gexp[side] = jnp.dot(jnp.concatenate(tiles, 0), select, preferred_element_type=F32)

    acc[...] = jnp.zeros_like(acc)
    project(s)
    for p in range(PIECES):
        for f in range(7):
            forward(p, f, theirs[p], t).wait_recv()
    project(t)
    loads[4].wait()

    def down(side, p, put):
        w = USED[p]

        def step(q, carry):
            wide = pl.ds(pl.multiple_of(q * QUARTER + p * WIDTH, 128), w)
            res = jnp.dot(hid[side], wd[:, wide], preferred_element_type=F32)
            res = res * jnp.concatenate([gexp[side]] * (w // 128), 1)
            base = axis_part(p, side, 0, q)
            for zz in range(4):
                for yy in range(4):
                    n = base + axis_part(p, side, 1, yy) + axis_part(p, side, 2, zz)
                    lo = (zz * 4 + yy) * ROWS
                    put(n, res[lo:lo + ROWS])
            return carry

        lax.fori_loop(0, 4, step, 0)

    def half_copy(p, h, n):
        b = lax.rem(lax.div(n, 32), 2)
        begin = (1 - b) * 32 if h == 0 else b * 32
        w = USED[p]
        return pltpu.make_async_remote_copy(
            src_ref=sib_out.at[p, rows_of(begin, 32), pl.ds(0, w)],
            dst_ref=sib_in.at[p, rows_of(begin, 32), pl.ds(0, w)],
            send_sem=rsib_send.at[p, h], recv_sem=rsib_recv.at[p, h],
            device_id=sibling, device_id_type=MESH)

    def rs_copy(p, k):
        region = pl.ds(SB_OFF[k], (1 << k) * ROWS)
        w = USED[p]
        return pltpu.make_async_remote_copy(
            src_ref=out_buf.at[p, region, pl.ds(0, w)], dst_ref=in_buf.at[p, region, pl.ds(0, w)],
            send_sem=rs_send.at[p, k], recv_sem=rs_recv.at[p, k],
            device_id=partner(p, k), device_id_type=MESH)

    for p in range(PIECES):
        def put_out(n, val):
            sib_out[p, rows_of(n, 1), :USED[p]] = val.astype(BF16)
        down(t, p, put_out)
        half_copy(p, 0, theirs[p]).start()
    for p in range(PIECES):
        half_copy(p, 1, theirs[p]).start()
    for p in range(PIECES):
        def put_total(n, val):
            total[p, rows_of(n, 1), :USED[p]] = val
        down(s, p, put_total)

    for p in range(PIECES):
        w = USED[p]
        half_copy(p, 0, own[p]).wait_recv()
        begin = start_of(other_of(own[p], 5), 5)

        def send_half(i, carry):
            at = rows_of(begin + i, 1)
            out_buf[p, pl.ds(pl.multiple_of(i * ROWS, ROWS), ROWS), :w] = (
                total[p, at, :w] + sib_in[p, at, :w].astype(F32)).astype(BF16)
            return carry

        lax.fori_loop(0, 32, send_half, 0)
        rs_copy(p, 5).start()
    for p in range(PIECES):
        w = USED[p]
        half_copy(p, 1, own[p]).wait_recv()
        begin = start_of(own[p], 5)

        def keep_half(i, carry):
            at = rows_of(begin + i, 1)
            total[p, at, :w] += sib_in[p, at, :w].astype(F32)
            return carry

        lax.fori_loop(0, 32, keep_half, 0)
    for k in range(4, -1, -1):
        for p in range(PIECES):
            w = USED[p]
            rs_copy(p, k + 1).wait_recv()
            outer = start_of(own[p], k + 1)
            away, keep = start_of(other_of(own[p], k), k), start_of(own[p], k)

            def send_part(i, carry):
                at = rows_of(away + i, 1)
                came = rows_of(SB_OFF[k + 1] // ROWS + away - outer + i, 1)
                here = pl.ds(pl.multiple_of(SB_OFF[k] + i * ROWS, ROWS), ROWS)
                out_buf[p, here, :w] = (
                    total[p, at, :w] + in_buf[p, came, :w].astype(F32)).astype(BF16)
                return carry

            def keep_part(i, carry):
                at = rows_of(keep + i, 1)
                came = rows_of(SB_OFF[k + 1] // ROWS + keep - outer + i, 1)
                total[p, at, :w] += in_buf[p, came, :w].astype(F32)
                return carry

            lax.fori_loop(0, 1 << k, send_part, 0)
            rs_copy(p, k).start()
            lax.fori_loop(0, 1 << k, keep_part, 0)

    pieces = []
    for p in range(PIECES):
        w = USED[p]
        rs_copy(p, 0).wait_recv()
        pieces.append((total[p, rows_of(own[p], 1), :w]
                       + in_buf[p, pl.ds(SB_OFF[0], ROWS), :w].astype(F32)).astype(BF16))
    pieces.append(jnp.zeros((ROWS, 256), BF16))
    result = jnp.concatenate(pieces, 1)

    row = lax.broadcasted_iota(jnp.int32, (64, 16), 0)
    col = lax.broadcasted_iota(jnp.int32, (64, 16), 1)
    packed = jnp.zeros((64, 512), F32)
    for c in range(4):
        hit = (((row >> 2) & 3) == c) & (col == (row >> 4) * 4 + (row & 3))
        packed += jnp.dot(jnp.where(hit, 1.0, 0.0).astype(BF16), result[:, 512 * c:512 * (c + 1)],
                          preferred_element_type=F32)
    pack2[...] = packed.astype(BF16).reshape(4, 16, 512)
    closed = a2a(pack2, got2, b2b_send, b2b_recv)
    for copy in closed:
        copy.wait()
    row = lax.broadcasted_iota(jnp.int32, (8, 16), 0)
    col = lax.broadcasted_iota(jnp.int32, (8, 16), 1)
    for j in range(4):
        for c in range(4):
            hit = (row < 4) & (col == c * 4 + row)
            value = jnp.dot(jnp.where(hit, 1.0, 0.0).astype(BF16), got2[j], preferred_element_type=F32)
            w = 512 if c < 3 else 256
            lo = QUARTER * j + 512 * c
            moe_out[:, lo:lo + w] = value[:4, :w].astype(BF16)

    for p in range(PIECES):
        for i in range(len(PLAN)):
            ag_copy(p, i).wait_send()
        for f in range(7):
            forward(p, f, own[p], s).wait_send()
        for h in range(2):
            half_copy(p, h, theirs[p]).wait_send()
        for k in range(STAGES):
            rs_copy(p, k).wait_send()
    for r in range(REQ):
        pltpu.make_async_copy(att.at[r], att_out.at[r], att_sem.at[r]).wait()


def per_device(tokens, routes, gates, w_gate, w_up, w_down, queries, cache, lengths):
    vmem = pl.BlockSpec(memory_space=pltpu.VMEM)
    smem = pl.BlockSpec(memory_space=pltpu.SMEM)
    hbm = pl.BlockSpec(memory_space=pl.ANY)
    dma = pltpu.SemaphoreType.DMA
    return pl.pallas_call(
        kernel,
        out_shape=(
            jax.ShapeDtypeStruct((REQ, D), BF16),
            jax.ShapeDtypeStruct((REQ, HEADS, LATENT), BF16),
        ),
        in_specs=[vmem, vmem, vmem, smem, hbm, hbm, hbm, hbm, hbm],
        out_specs=(vmem, hbm),
        scratch_shapes=[
            pltpu.VMEM((2, PIECES, BLOCKS * ROWS, WIDTH), BF16),
            pltpu.VMEM((D, UNITS), BF16),
            pltpu.VMEM((D, UNITS), BF16),
            pltpu.VMEM((UNITS, D), BF16),
            pltpu.VMEM((REQ, MAX_LEN, KEY), BF16),
            pltpu.VMEM((REQ, HEADS, KEY), BF16),
            pltpu.VMEM((REQ, HEADS, LATENT), BF16),
            pltpu.VMEM((2, 256, 2 * UNITS), F32),
            pltpu.VMEM((2, 256, UNITS), BF16),
            pltpu.VMEM((2, 256, 128), F32),
            pltpu.VMEM((PIECES, BLOCKS * ROWS, WIDTH), F32),
            pltpu.VMEM((PIECES, BLOCKS * ROWS, WIDTH), BF16),
            pltpu.VMEM((PIECES, BLOCKS * ROWS, WIDTH), BF16),
            pltpu.VMEM((PIECES, 1008, WIDTH), BF16),
            pltpu.VMEM((PIECES, 1008, WIDTH), BF16),
            pltpu.VMEM((4, 16, 512), BF16),
            pltpu.VMEM((4, 16, 512), BF16),
            pltpu.VMEM((4, 16, 512), BF16),
            pltpu.VMEM((4, 16, 512), BF16),
            dma((5,)), dma((REQ,)), dma((3,)), dma((3,)),
            dma((PIECES, len(PLAN))), dma((PIECES, len(PLAN))),
            dma((PIECES, 7)), dma((PIECES, 7)),
            dma((PIECES, 2)), dma((PIECES, 2)),
            dma((PIECES, STAGES)), dma((PIECES, STAGES)),
            dma((3,)), dma((3,)),
        ],
        compiler_params=pltpu.CompilerParams(
            collective_id=0, has_side_effects=True, vmem_limit_bytes=60 * 1024 * 1024),
    )(tokens, routes, gates, lengths, w_gate, w_up, w_down, queries, cache)


def solution(mesh):
    a = ("side", "dev")
    in_specs = (P(a, None),) * 3 + (P(a, None, None),) * 5 + (P(a),)
    out_specs = (P(a, None), P(a, None, None))
    return jax.shard_map(
        per_device, mesh=mesh, in_specs=in_specs, out_specs=out_specs, check_vma=False
    )
```

time: 527 us -> 110 us (0.21)
  blocking collectives: 320 us -> 0 us
  waiting for transfers between devices: 144 us -> 0 us
  Pallas kernels: 0 us -> 95.2 us
  matrix products: 31.4 us -> 0 us
  between operations: 14.1 us -> 0.64 us
    all_gather x1 -> x0, blocking collectives: 320 us -> none  [per_device(): weight = lax.all_gather(dense, axes, axis=0, tiled=True)]
    unnamed x3 -> x0, waiting for transfers between devices: 144 us -> none
    pallas_call x0 -> x1, Pallas kernels: none -> 95.2 us  [per_device(): pl.pallas_call(kernel, out_shape=(jax.ShapeDtypeStruct((REQ, D), BF16), j...]
    dot_general x3 -> x0, matrix products: 26.8 us -> none  [the longest x1 16 us: per_device(): jnp.dot(hidden, w_down[0], preferred_element_type=jnp.float32)]
    unnamed x6 -> x4, local copies, waits for them, and re-layouts: 14.3 us -> 13.2 us
  transfers between devices with their start and end apart: 2 -> 0, of which waited for: 1 -> 0; matrix products, arithmetic and copies ran while one was open for 2% -> 0% of each run, Pallas kernels for 0% -> 0%
where the time goes in v2:
time: 110 us; the launch traced here: 109 us
  Pallas kernels  95.2 us (87%)
  local copies, waits for them, and re-layouts  13.2 us (12%)
    pallas_call x1, Pallas kernels, per_device(): pl.pallas_call(kernel, out_shape=(jax.ShapeDtypeStruct((REQ, D), BF16), j...  95.2 us
    unnamed x4, local copies, waits for them, and re-layouts  13.2 us

profile of v2, /device:TPU:0, one launch (start us, length us, event | category | flops | bytes accessed | tf_op | source)
XLA Modules:
  0.0 109.1 jit_solution(1058172664164374064)
XLA Ops:
  0.6 2.2 %copy.11.queries = bf16[4,128,576]{2,1,0:T(8,128)(2,1)} copy(bf16[4,128,576]{1,2,0:T(8,128)(2,1)} %param.15) | data formatting | bytes 1179648 | tf_op args[6]
  2.8 7.7 %copy.12.cache = bf16[4,1024,576]{2,1,0:T(8,128)(2,1)} copy(bf16[4,1024,576]{1,2,0:T(8,128)(2,1)} %param.16) | data formatting | bytes 9437184 | tf_op args[7]
  10.5 95.2 %shard_map.104 = (bf16[4,7168]{1,0:T(4,128)(2,1)}, bf16[4,128,512]{2,1,0:T(8,128)(2,1)}) custom-call(bf16[4,7168]{1,0:T(4,128)(2,1)} %tokens.1, s32[4,8]{1,0:T(4,128)} %routes.1, f32[4,8]{1,0:T(4,128)} %gates.1, s32[4]{0:T(128)} %lengths.1, bf16[1,7168,256]{2,1,0:T(8,128)(2,1)} %w_gate.1, bf16[1,7168,256]{2,1,0:T(8,128)(2,1)} %w_up.1, ...), custom_call_target="tpu_custom_call" | custom-call | tf_op jit(solution)/shard_map/pallas_call | solution.py:439
  105.7 1.5 %copy.15 = bf16[4,7168]{1,0:T(4,128)(2,1)} copy(bf16[4,7168]{1,0:T(4,128)(2,1)} %get-tuple-element.4) | data formatting | bytes 114688
  107.2 1.9 %copy.16 = bf16[4,128,512]{2,1,0:T(8,128)(2,1)} copy(bf16[4,128,512]{2,1,0:T(8,128)(2,1)} %get-tuple-element.5) | data formatting | bytes 1048576

commit v3 on v2

v3 whole, which is shorter than its diff:
```python
import jax
import jax.numpy as jnp
from jax import lax
from jax.experimental import pallas as pl
from jax.experimental.pallas import tpu as pltpu
from jax.sharding import PartitionSpec as P

D = 7168
UNITS = 256
LATENT = 512
KEY = 576
HEADS = 128
MAX_LEN = 1024
REQ = 4
EXPERTS = 16
SCALE = 192.0 ** -0.5

QUARTER = 1792
PIECES = 3
WIDTH = 640
USED = (640, 640, 512)
ROWS = 16
BLOCKS = 64
GROUP = 8
MESH = pl.DeviceIdType.MESH
F32 = jnp.float32
BF16 = jnp.bfloat16


PLAN = ((3, 0, 0), (3, 0, 1), (4, 0, 0), (4, 0, 1), (5, 0, None), (4, 1, None), (5, 1, None),
        (5, 2, None), (5, 3, None))
NEAR = {3: 1, 4: 2, 5: 4}
RETURN = ((5, 4), (5, 5), (5, 6), (5, 7), (4, 2), (4, 3), (3, 1))


def beta_of(p, k, s):
    return s if k < 3 else 1 - s


def bit_of(c, beta):
    if isinstance(c, int):
        high, low = c // 2, ((c + 1) // 2) % 2
    else:
        high, low = lax.div(c, 2), lax.rem(lax.div(c + 1, 2), 2)
    return beta * high + (1 - beta) * low


def flip_of(c, beta):
    return beta * (3 - c) + (1 - beta) * (c + 1 - 2 * lax.rem(c, 2))


def axis_part(p, s, a, c):
    return bit_of(c, s) * (1 << a) + bit_of(c, 1 - s) * (GROUP << ((a - p) % 3))


def block_of(p, s, x, y, z):
    return axis_part(p, s, 0, x) + axis_part(p, s, 1, y) + axis_part(p, s, 2, z)


def flip_bits(n, mask):
    out = n
    for k in range(3):
        if mask >> k & 1:
            out = out + (1 << k) * (1 - 2 * lax.rem(lax.div(n, 1 << k), 2))
    return out


def kernel(
    tokens, routes, gates, lengths, w_gate, w_up, w_down, queries, cache,
    moe_out, att_out,
    x_buf, wg, wu, wd, kv, qs, att, acc, hid, gexp, total, sib_out, sib_in, out_buf, in_buf,
    pack, got, pack2, got2, cube, cube_out, cube_in,
    local_sem, att_sem, a2a_send, a2a_recv, cube_send, cube_recv, ag_send, ag_recv, sib_send, sib_recv,
    rsib_send, rsib_recv, rs_send, rs_recv, back_send, back_recv, b2b_send, b2b_recv,
):
    s = lax.axis_index("side")
    dev = lax.axis_index("dev")
    x, y, z = lax.rem(dev, 4), lax.rem(lax.div(dev, 4), 4), lax.div(dev, 16)
    coords = (x, y, z)
    t = 1 - s

    def chip(cx, cy, cz):
        return cz * 16 + cy * 4 + cx

    def moved(mask, beta):
        return (s, chip(*[flip_of(c, beta) if mask >> a & 1 else c for a, c in enumerate(coords)]))

    def partner(p, k):
        return moved(1 << ((k + p) % 3), 1 - s)

    peers = [(s, chip(lax.rem(x + d, 4), y, z)) for d in (1, 2, 3)]
    sibling = (t, dev)

    loads = [
        pltpu.make_async_copy(queries, qs, local_sem.at[0]),
        pltpu.make_async_copy(cache, kv, local_sem.at[1]),
        pltpu.make_async_copy(w_gate.at[0], wg, local_sem.at[2]),
        pltpu.make_async_copy(w_up.at[0], wu, local_sem.at[3]),
        pltpu.make_async_copy(w_down.at[0], wd, local_sem.at[4]),
    ]

    barrier = pltpu.get_barrier_semaphore()
    greet = [(s, chip(lax.rem(x + 2, 4), y, z)), sibling]
    greet += [moved(mask, s) for mask in range(1, 8)]
    greet += [moved(1 << a, 1 - s) for a in range(3)]
    for who in greet:
        pl.semaphore_signal(barrier, inc=1, device_id=who, device_id_type=MESH)
    for load in loads:
        load.start()

    lane = lax.broadcasted_iota(jnp.int32, (4, 128), 1)
    dense = jnp.zeros((4, 128), F32)
    for k in range(8):
        dense += jnp.where(routes[:, k:k + 1] == (lane & 15), gates[:, k:k + 1], 0.0)
    first = dense.astype(BF16).astype(F32)
    second = (dense - first).astype(BF16).astype(F32)
    third = dense - first - second
    aux = jnp.where(lane < 16, first, jnp.where(lane < 32, second, jnp.where(lane < 48, third, 0.0)))
    aux = jnp.concatenate([aux, jnp.zeros((4, 128), F32)], 1)
    for j in range(4):
        parts = []
        for c in range(4):
            lo = QUARTER * j + 512 * c
            if c < 3:
                parts.append(tokens[:, lo:lo + 512].astype(F32))
            else:
                parts.append(jnp.concatenate([tokens[:, lo:lo + 256].astype(F32), aux], 1))
        pack[j] = jnp.concatenate(parts, 0).astype(BF16)

    pl.semaphore_wait(barrier, len(greet))

    def a2a(src, dst, send, recv):
        copies = []
        for i, who in enumerate(peers):
            to = lax.rem(x + i + 1, 4)
            copies.append(pltpu.make_async_remote_copy(
                src_ref=src.at[to], dst_ref=dst.at[x], send_sem=send.at[i], recv_sem=recv.at[i],
                device_id=who, device_id_type=MESH))
        for copy in copies:
            copy.start()
        dst[x] = src[x]
        return copies

    opened = a2a(pack, got, a2a_send, a2a_recv)
    for copy in opened:
        copy.wait()
    rows = got[...].reshape(64, 512)
    row = lax.broadcasted_iota(jnp.int32, (16, 64), 0)
    col = lax.broadcasted_iota(jnp.int32, (16, 64), 1)
    assembled = []
    for c in range(4):
        select = jnp.where(col == (row >> 2) * 16 + c * 4 + (row & 3), 1.0, 0.0).astype(BF16)
        assembled.append(jnp.dot(select, rows, preferred_element_type=F32).astype(BF16))
    assembled = jnp.concatenate(assembled, 1)

    own = [block_of(p, s, x, y, z) for p in range(PIECES)]
    theirs = [block_of(p, t, x, y, z) for p in range(PIECES)]
    low = lax.rem(own[0], GROUP)
    high = [lax.div(n, GROUP) for n in own]
    high_theirs = [lax.div(n, GROUP) for n in theirs]
    cube[low] = assembled[:, :PIECES * WIDTH]

    def cube_copy(mask):
        return pltpu.make_async_remote_copy(
            src_ref=cube.at[low], dst_ref=cube.at[low],
            send_sem=cube_send.at[mask - 1], recv_sem=cube_recv.at[mask - 1],
            device_id=moved(mask, s), device_id_type=MESH)

    def cube_arrival(mask):
        came = cube.at[flip_bits(low, mask)]
        return pltpu.make_async_remote_copy(
            src_ref=came, dst_ref=came,
            send_sem=cube_send.at[mask - 1], recv_sem=cube_recv.at[mask - 1],
            device_id=moved(mask, s), device_id_type=MESH)

    def half_start(h):
        mine = lax.div(low, 4)
        return 4 * (mine if h == 0 else 1 - mine)

    def ag_copy(p, i):
        k, unit, h = PLAN[i]
        begin, size = (0, 8) if h is None else (half_start(h), 4)
        dst = x_buf.at[s, p, pl.ds(flip_bits(high[p], unit) * GROUP + begin, size)]
        if unit == 0:
            src = cube.at[pl.ds(begin, size), :, pl.ds(p * WIDTH, WIDTH)]
        else:
            src = dst
        return pltpu.make_async_remote_copy(
            src_ref=src, dst_ref=dst, send_sem=ag_send.at[p, i], recv_sem=ag_recv.at[p, i],
            device_id=partner(p, k), device_id_type=MESH)

    def ag_arrival(p, i):
        k, unit, h = PLAN[i]
        begin, size = (0, 8) if h is None else (4 * h, 4)
        came = x_buf.at[s, p, pl.ds(flip_bits(high[p], unit ^ NEAR[k]) * GROUP + begin, size)]
        return pltpu.make_async_remote_copy(
            src_ref=came, dst_ref=came, send_sem=ag_send.at[p, i], recv_sem=ag_recv.at[p, i],
            device_id=partner(p, k), device_id_type=MESH)

    def forward(p, unit, top, side):
        region = x_buf.at[side, p, pl.ds(flip_bits(top, unit) * GROUP, GROUP)]
        return pltpu.make_async_remote_copy(
            src_ref=region, dst_ref=region, send_sem=sib_send.at[p, unit], recv_sem=sib_recv.at[p, unit],
            device_id=sibling, device_id_type=MESH)

    def attend(r):
        scores = jnp.dot(qs[r].T, kv[r], preferred_element_type=F32) * SCALE
        valid = lax.broadcasted_iota(jnp.int32, (HEADS, MAX_LEN), 1) < lengths[r]
        scores = jnp.where(valid, scores, -1e30)
        highest = jnp.max(scores, -1, keepdims=True)
        weights = jnp.where(valid, jnp.exp(scores - highest), 0.0)
        chance = (weights / jnp.sum(weights, -1, keepdims=True)).astype(BF16)
        att[r] = lax.dot_general(
            chance, kv[r, :LATENT, :], (((1,), (1,)), ((), ())), preferred_element_type=F32).astype(BF16)
        pltpu.make_async_copy(att.at[r], att_out.at[r], att_sem.at[r]).start()

    acc[...] = jnp.zeros_like(acc)
    for mask in (7, 3, 5, 6, 1, 2, 4):
        cube_copy(mask).start()
    loads[0].wait()
    loads[1].wait()
    attend(0)
    attend(1)
    for mask in (1, 2, 3):
        cube_arrival(mask).wait_recv()
    for i in (0, 2):
        for p in range(PIECES):
            ag_copy(p, i).start()
    attend(2)
    for mask in (4, 5, 6, 7):
        cube_arrival(mask).wait_recv()
    for i in (1, 3, 4):
        for p in range(PIECES):
            ag_copy(p, i).start()
    for p in range(PIECES):
        x_buf[s, p, pl.ds(high[p] * GROUP, GROUP)] = cube[:, :, WIDTH * p:WIDTH * (p + 1)]
    for p in range(PIECES):
        forward(p, 0, high[p], s).start()
    attend(3)
    for arrived, unit, sent in (((0, 1), 1, (5, 6)), ((2, 3), 2, (7,)), ((5,), 3, (8,))):
        for p in range(PIECES):
            for i in arrived:
                ag_arrival(p, i).wait_recv()
            for i in sent:
                ag_copy(p, i).start()
            forward(p, unit, high[p], s).start()

    def two_of(side, b):
        beta = 1 - side
        return (beta * 2 * b + (1 - beta) * b, beta * (2 * b + 1) + (1 - beta) * (3 - b))

    def project(side, p, b):
        w = USED[p]
        every = (0, 1, 2, 3)
        pair = two_of(side, b)
        zs = pair if p == 0 else every
        ys = pair if p == 2 else every

        def step(i, carry):
            q = pair[0] + i * (pair[1] - pair[0]) if p == 1 else i
            base = axis_part(p, side, 0, q)
            tiles = [
                x_buf[side, p, base + axis_part(p, side, 1, yy) + axis_part(p, side, 2, zz), :, :w]
                for zz in zs for yy in ys]
            lhs = jnp.concatenate(tiles, 0)
            deep = pl.ds(pl.multiple_of(q * QUARTER + p * WIDTH, 128), w)
            for weight, lo in ((wg, 0), (wu, UNITS)):
                res = jnp.dot(lhs, weight[deep, :], preferred_element_type=F32)
                for m, zz in enumerate(zs):
                    for n, yy in enumerate(ys):
                        r = (m * len(ys) + n) * ROWS
                        acc[side, zz * 4 + yy, :, lo:lo + UNITS] += res[r:r + ROWS]
            return carry

        lax.fori_loop(0, 2 if p == 1 else 4, step, 0)

    def bit5(p, side):
        return bit_of(coords[(5 + p) % 3], 1 - side)

    loads[2].wait()
    loads[3].wait()
    for p in range(PIECES):
        project(s, p, bit5(p, s))
    for p in range(PIECES):
        for unit in range(4):
            forward(p, unit, high_theirs[p], t).wait_recv()
        project(t, p, bit5(p, t))
    for unit, i in ((4, 4), (5, 6), (6, 7), (7, 8)):
        for p in range(PIECES):
            ag_arrival(p, i).wait_recv()
            forward(p, unit, high[p], s).start()
    for p in range(PIECES):
        project(s, p, 1 - bit5(p, s))
    for p in range(PIECES):
        for unit in range(4, 8):
            forward(p, unit, high_theirs[p], t).wait_recv()
        project(t, p, 1 - bit5(p, t))

    expert = s * 8 + z * 2 + lax.div(y, 2)
    deep_lane = lax.broadcasted_iota(jnp.int32, (128, 128), 0)
    select = jnp.where(((deep_lane & 15) == expert) & (deep_lane < 48), 1.0, 0.0).astype(BF16)
    for side in (t, s):
        both = acc[side].reshape(256, 2 * UNITS)
        gate, upper = both[:, :UNITS], both[:, UNITS:]
        hid[side] = (gate / (1.0 + jnp.exp(-gate)) * upper).astype(BF16)
        tiles = [
            x_buf[side, 2, axis_part(2, side, 1, yy) + axis_part(2, side, 2, zz), :, 512:640]
            for zz in range(4) for yy in range(4)]
        gexp[side] = jnp.dot(jnp.concatenate(tiles, 0), select, preferred_element_type=F32)
    loads[4].wait()

    def down(side, p, put):
        w = USED[p]

        def step(q, carry):
            wide = pl.ds(pl.multiple_of(q * QUARTER + p * WIDTH, 128), w)
            res = jnp.dot(hid[side], wd[:, wide], preferred_element_type=F32)
            res = res * jnp.concatenate([gexp[side]] * (w // 128), 1)
            base = axis_part(p, side, 0, q)
            for zz in range(4):
                for yy in range(4):
                    n = base + axis_part(p, side, 1, yy) + axis_part(p, side, 2, zz)
                    lo = (zz * 4 + yy) * ROWS
                    put(n, res[lo:lo + ROWS])
            return carry

        lax.fori_loop(0, 4, step, 0)

    def half_copy(p, h, n):
        b = lax.div(n, 32)
        begin = (1 - b) * 32 if h == 0 else b * 32
        w = USED[p]
        return pltpu.make_async_remote_copy(
            src_ref=sib_out.at[p, pl.ds(begin, 32), :, pl.ds(0, w)],
            dst_ref=sib_in.at[p, pl.ds(begin, 32), :, pl.ds(0, w)],
            send_sem=rsib_send.at[p, h], recv_sem=rsib_recv.at[p, h],
            device_id=sibling, device_id_type=MESH)

    def rs_copy(p, i):
        w = USED[p]
        return pltpu.make_async_remote_copy(
            src_ref=out_buf.at[p, i, :, :, pl.ds(0, w)], dst_ref=in_buf.at[p, i, :, :, pl.ds(0, w)],
            send_sem=rs_send.at[p, i], recv_sem=rs_recv.at[p, i],
            device_id=partner(p, RETURN[i][0]), device_id_type=MESH)

    def came_for(unit):
        return [] if unit > 3 else [unit] + ([4 + unit] if unit < 2 else []) + ([6] if unit < 1 else [])

    def summed(p, unit, j):
        w = USED[p]
        n = flip_bits(high[p], unit) * GROUP + j
        value = total[p, n, :, :w] + sib_in[p, n, :, :w].astype(F32)
        for slot in came_for(unit):
            value += in_buf[p, slot, j, :, :w].astype(F32)
        return value

    def give(p, i):
        def step(j, carry):
            out_buf[p, i, j, :, :USED[p]] = summed(p, RETURN[i][1], j).astype(BF16)
            return carry

        lax.fori_loop(0, GROUP, step, 0)
        rs_copy(p, i).start()

    for p in range(PIECES):
        def put_out(n, val):
            sib_out[p, n, :, :USED[p]] = val.astype(BF16)
        down(t, p, put_out)
        half_copy(p, 0, theirs[p]).start()
    for p in range(PIECES):
        half_copy(p, 1, theirs[p]).start()
    for p in range(PIECES):
        def put_total(n, val):
            total[p, n, :, :USED[p]] = val
        down(s, p, put_total)
        half_copy(p, 0, own[p]).wait_recv()
        for i in (3, 2, 1, 0):
            give(p, i)
    for p in range(PIECES):
        half_copy(p, 1, own[p]).wait_recv()
    for i, before in ((5, (3,)), (4, (2,)), (6, (1, 5))):
        for p in range(PIECES):
            for slot in before:
                rs_copy(p, slot).wait_recv()
            give(p, i)
    for p in range(PIECES):
        for slot in (0, 4, 6):
            rs_copy(p, slot).wait_recv()

    def back_copy(mask):
        return pltpu.make_async_remote_copy(
            src_ref=cube_out.at[flip_bits(low, mask)], dst_ref=cube_in.at[low],
            send_sem=back_send.at[mask - 1], recv_sem=back_recv.at[mask - 1],
            device_id=moved(mask, s), device_id_type=MESH)

    def back_arrival(mask):
        came = cube_in.at[flip_bits(low, mask)]
        return pltpu.make_async_remote_copy(
            src_ref=came, dst_ref=came,
            send_sem=back_send.at[mask - 1], recv_sem=back_recv.at[mask - 1],
            device_id=moved(mask, s), device_id_type=MESH)

    for mask in (7, 3, 5, 6, 1, 2, 4):
        to = flip_bits(low, mask)
        for p in range(PIECES):
            cube_out[to, :, WIDTH * p:WIDTH * p + USED[p]] = summed(p, 0, to).astype(BF16)
        back_copy(mask).start()
    result = jnp.concatenate([summed(p, 0, low) for p in range(PIECES)], 1)
    for mask in (4, 2, 1, 6, 5, 3, 7):
        back_arrival(mask).wait_recv()
        result += cube_in[flip_bits(low, mask)].astype(F32)
    result = jnp.concatenate([result.astype(BF16), jnp.zeros((ROWS, 256), BF16)], 1)

    row = lax.broadcasted_iota(jnp.int32, (64, 16), 0)
    col = lax.broadcasted_iota(jnp.int32, (64, 16), 1)
    packed = jnp.zeros((64, 512), F32)
    for c in range(4):
        hit = (((row >> 2) & 3) == c) & (col == (row >> 4) * 4 + (row & 3))
        packed += jnp.dot(jnp.where(hit, 1.0, 0.0).astype(BF16), result[:, 512 * c:512 * (c + 1)],
                          preferred_element_type=F32)
    pack2[...] = packed.astype(BF16).reshape(4, 16, 512)
    closed = a2a(pack2, got2, b2b_send, b2b_recv)
    for copy in closed:
        copy.wait()
    row = lax.broadcasted_iota(jnp.int32, (8, 16), 0)
    col = lax.broadcasted_iota(jnp.int32, (8, 16), 1)
    for j in range(4):
        for c in range(4):
            hit = (row < 4) & (col == c * 4 + row)
            value = jnp.dot(jnp.where(hit, 1.0, 0.0).astype(BF16), got2[j], preferred_element_type=F32)
            w = 512 if c < 3 else 256
            lo = QUARTER * j + 512 * c
            moe_out[:, lo:lo + w] = value[:4, :w].astype(BF16)

    for mask in range(1, 8):
        cube_copy(mask).wait_send()
        back_copy(mask).wait_send()
    for p in range(PIECES):
        for i in range(len(PLAN)):
            ag_copy(p, i).wait_send()
        for unit in range(8):
            forward(p, unit, high[p], s).wait_send()
        for h in range(2):
            half_copy(p, h, theirs[p]).wait_send()
        for i in range(len(RETURN)):
            rs_copy(p, i).wait_send()
    for r in range(REQ):
        pltpu.make_async_copy(att.at[r], att_out.at[r], att_sem.at[r]).wait()


def per_device(tokens, routes, gates, w_gate, w_up, w_down, queries, cache, lengths):
    vmem = pl.BlockSpec(memory_space=pltpu.VMEM)
    smem = pl.BlockSpec(memory_space=pltpu.SMEM)
    hbm = pl.BlockSpec(memory_space=pl.ANY)
    dma = pltpu.SemaphoreType.DMA
    return pl.pallas_call(
        kernel,
        out_shape=(
            jax.ShapeDtypeStruct((REQ, D), BF16),
            jax.ShapeDtypeStruct((REQ, HEADS, LATENT), BF16),
        ),
        in_specs=[vmem, vmem, vmem, smem, hbm, hbm, hbm, hbm, hbm],
        out_specs=(vmem, hbm),
        scratch_shapes=[
            pltpu.VMEM((2, PIECES, BLOCKS, ROWS, WIDTH), BF16),
            pltpu.VMEM((D, UNITS), BF16),
            pltpu.VMEM((D, UNITS), BF16),
            pltpu.VMEM((UNITS, D), BF16),
            pltpu.VMEM((REQ, KEY, MAX_LEN), BF16),
            pltpu.VMEM((REQ, KEY, HEADS), BF16),
            pltpu.VMEM((REQ, HEADS, LATENT), BF16),
            pltpu.VMEM((2, 16, ROWS, 2 * UNITS), F32),
            pltpu.VMEM((2, 256, UNITS), BF16),
            pltpu.VMEM((2, 256, 128), F32),
            pltpu.VMEM((PIECES, BLOCKS, ROWS, WIDTH), F32),
            pltpu.VMEM((PIECES, BLOCKS, ROWS, WIDTH), BF16),
            pltpu.VMEM((PIECES, BLOCKS, ROWS, WIDTH), BF16),
            pltpu.VMEM((PIECES, len(RETURN), GROUP, ROWS, WIDTH), BF16),
            pltpu.VMEM((PIECES, len(RETURN), GROUP, ROWS, WIDTH), BF16),
            pltpu.VMEM((4, 16, 512), BF16),
            pltpu.VMEM((4, 16, 512), BF16),
            pltpu.VMEM((4, 16, 512), BF16),
            pltpu.VMEM((4, 16, 512), BF16),
            pltpu.VMEM((GROUP, ROWS, PIECES * WIDTH), BF16),
            pltpu.VMEM((GROUP, ROWS, QUARTER), BF16),
            pltpu.VMEM((GROUP, ROWS, QUARTER), BF16),
            dma((5,)), dma((REQ,)), dma((3,)), dma((3,)), dma((7,)), dma((7,)),
            dma((PIECES, len(PLAN))), dma((PIECES, len(PLAN))),
            dma((PIECES, 8)), dma((PIECES, 8)),
            dma((PIECES, 2)), dma((PIECES, 2)),
            dma((PIECES, len(RETURN))), dma((PIECES, len(RETURN))), dma((7,)), dma((7,)),
            dma((3,)), dma((3,)),
        ],
        compiler_params=pltpu.CompilerParams(
            collective_id=0, has_side_effects=True, vmem_limit_bytes=60 * 1024 * 1024),
    )(tokens, routes, gates, lengths, w_gate, w_up, w_down,
      queries.transpose(0, 2, 1), cache.transpose(0, 2, 1))


def solution(mesh):
    a = ("side", "dev")
    in_specs = (P(a, None),) * 3 + (P(a, None, None),) * 5 + (P(a),)
    out_specs = (P(a, None), P(a, None, None))
    return jax.shard_map(
        per_device, mesh=mesh, in_specs=in_specs, out_specs=out_specs, check_vma=False
    )
```

time: 110 us -> 80.4 us (0.73)
  Pallas kernels: 95.2 us -> 76.2 us
  local copies, waits for them, and re-layouts: 13.2 us -> 3.33 us
    pallas_call x1, Pallas kernels: 95.2 us -> 76.2 us  [per_device(): pl.pallas_call(kernel, out_shape=(jax.ShapeDtypeStruct((REQ, D), BF16), j...]
    unnamed x4 -> x2, local copies, waits for them, and re-layouts: 13.2 us -> 3.33 us
where the time goes in v3:
time: 80.4 us; the launch traced here: 80.2 us
  Pallas kernels  76.2 us (95%)
  local copies, waits for them, and re-layouts  3.33 us (4%)
    pallas_call x1, Pallas kernels, per_device(): pl.pallas_call(kernel, out_shape=(jax.ShapeDtypeStruct((REQ, D), BF16), j...  76.2 us
    unnamed x2, local copies, waits for them, and re-layouts  3.33 us

profile of v3, /device:TPU:0, one launch (start us, length us, event | category | flops | bytes accessed | tf_op | source)
XLA Modules:
  0.0 80.2 jit_solution(10511136012125126692)
XLA Ops:
  0.6 76.2 %shard_map.104 = (bf16[4,7168]{1,0:T(4,128)(2,1)}, bf16[4,128,512]{2,1,0:T(8,128)(2,1)}) custom-call(bf16[4,7168]{1,0:T(4,128)(2,1)} %tokens.1, s32[4,8]{1,0:T(4,128)} %routes.1, f32[4,8]{1,0:T(4,128)} %gates.1, s32[4]{0:T(128)} %lengths.1, bf16[1,7168,256]{2,1,0:T(8,128)(2,1)} %w_gate.1, bf16[1,7168,256]{2,1,0:T(8,128)(2,1)} %w_up.1, ...), custom_call_target="tpu_custom_call" | custom-call | tf_op jit(solution)/shard_map/pallas_call | solution.py:456
  76.8 1.5 %copy.13 = bf16[4,7168]{1,0:T(4,128)(2,1)} copy(bf16[4,7168]{1,0:T(4,128)(2,1)} %get-tuple-element.4) | data formatting | bytes 114688
  78.3 1.9 %copy.14 = bf16[4,128,512]{2,1,0:T(8,128)(2,1)} copy(bf16[4,128,512]{2,1,0:T(8,128)(2,1)} %get-tuple-element.5) | data formatting | bytes 1048576

commit v4 on v3

--- a/solution.py
+++ b/solution.py
@@ -17,6 +17,7 @@
 
 QUARTER = 1792
 PIECES = 3
+UNROLL = True
 WIDTH = 640
 USED = (640, 640, 512)
 ROWS = 16
@@ -27,8 +28,8 @@
 BF16 = jnp.bfloat16
 
 
-PLAN = ((3, 0, 0), (3, 0, 1), (4, 0, 0), (4, 0, 1), (5, 0, None), (4, 1, None), (5, 1, None),
-        (5, 2, None), (5, 3, None))
+PLAN = ((3, 0, 0), (3, 0, 1), (4, 0, 0), (4, 0, 1), (5, 0, 0), (4, 1, None), (5, 1, None),
+        (5, 2, None), (5, 3, None), (5, 0, 1))
 NEAR = {3: 1, 4: 2, 5: 4}
 RETURN = ((5, 4), (5, 5), (5, 6), (5, 7), (4, 2), (4, 3), (3, 1))
 
@@ -67,9 +68,9 @@
 
 def kernel(
     tokens, routes, gates, lengths, w_gate, w_up, w_down, queries, cache,
-    moe_out, att_out,
+    got2, att_out,
     x_buf, wg, wu, wd, kv, qs, att, acc, hid, gexp, total, sib_out, sib_in, out_buf, in_buf,
-    pack, got, pack2, got2, cube, cube_out, cube_in,
+    pack, got, pack2, cube, cube_out, cube_in,
     local_sem, att_sem, a2a_send, a2a_recv, cube_send, cube_recv, ag_send, ag_recv, sib_send, sib_recv,
     rsib_send, rsib_recv, rs_send, rs_recv, back_send, back_recv, b2b_send, b2b_recv,
 ):
@@ -215,7 +216,7 @@
         pltpu.make_async_copy(att.at[r], att_out.at[r], att_sem.at[r]).start()
 
     acc[...] = jnp.zeros_like(acc)
-    for mask in (7, 3, 5, 6, 1, 2, 4):
+    for mask in (3, 1, 2, 7, 5, 6, 4):
         cube_copy(mask).start()
     loads[0].wait()
     loads[1].wait()
@@ -223,13 +224,13 @@
     attend(1)
     for mask in (1, 2, 3):
         cube_arrival(mask).wait_recv()
-    for i in (0, 2):
+    for i in (0, 2, 4):
         for p in range(PIECES):
             ag_copy(p, i).start()
     attend(2)
     for mask in (4, 5, 6, 7):
         cube_arrival(mask).wait_recv()
-    for i in (1, 3, 4):
+    for i in (1, 3, 9):
         for p in range(PIECES):
             ag_copy(p, i).start()
     for p in range(PIECES):
@@ -272,7 +273,7 @@
                         acc[side, zz * 4 + yy, :, lo:lo + UNITS] += res[r:r + ROWS]
             return carry
 
-        lax.fori_loop(0, 2 if p == 1 else 4, step, 0)
+        lax.fori_loop(0, 2 if p == 1 else 4, step, 0, unroll=UNROLL)
 
     def bit5(p, side):
         return bit_of(coords[(5 + p) % 3], 1 - side)
@@ -285,9 +286,10 @@
         for unit in range(4):
             forward(p, unit, high_theirs[p], t).wait_recv()
         project(t, p, bit5(p, t))
-    for unit, i in ((4, 4), (5, 6), (6, 7), (7, 8)):
+    for unit, arrived in ((4, (4, 9)), (5, (6,)), (6, (7,)), (7, (8,))):
         for p in range(PIECES):
-            ag_arrival(p, i).wait_recv()
+            for i in arrived:
+                ag_arrival(p, i).wait_recv()
             forward(p, unit, high[p], s).start()
     for p in range(PIECES):
         project(s, p, 1 - bit5(p, s))
@@ -302,29 +304,36 @@
     for side in (t, s):
         both = acc[side].reshape(256, 2 * UNITS)
         gate, upper = both[:, :UNITS], both[:, UNITS:]
-        hid[side] = (gate / (1.0 + jnp.exp(-gate)) * upper).astype(BF16)
+        hid[side] = (gate / (1.0 + jnp.exp(-gate)) * upper).astype(BF16).reshape(16, ROWS, UNITS)
         tiles = [
             x_buf[side, 2, axis_part(2, side, 1, yy) + axis_part(2, side, 2, zz), :, 512:640]
             for zz in range(4) for yy in range(4)]
-        gexp[side] = jnp.dot(jnp.concatenate(tiles, 0), select, preferred_element_type=F32)
+        gexp[side] = jnp.dot(
+            jnp.concatenate(tiles, 0), select, preferred_element_type=F32).reshape(16, ROWS, 128)
     loads[4].wait()
 
-    def down(side, p, put):
+    def down(side, p, b, put):
         w = USED[p]
-
-        def step(q, carry):
+        every = (0, 1, 2, 3)
+        pair = two_of(side, b)
+        zs = pair if p == 0 else every
+        ys = pair if p == 2 else every
+        lhs = jnp.concatenate([hid[side, zz * 4 + yy] for zz in zs for yy in ys], 0)
+        share = jnp.concatenate([gexp[side, zz * 4 + yy] for zz in zs for yy in ys], 0)
+        share = jnp.concatenate([share] * (w // 128), 1)
+
+        def step(i, carry):
+            q = pair[0] + i * (pair[1] - pair[0]) if p == 1 else i
             wide = pl.ds(pl.multiple_of(q * QUARTER + p * WIDTH, 128), w)
-            res = jnp.dot(hid[side], wd[:, wide], preferred_element_type=F32)
-            res = res * jnp.concatenate([gexp[side]] * (w // 128), 1)
+            res = jnp.dot(lhs, wd[:, wide], preferred_element_type=F32) * share
             base = axis_part(p, side, 0, q)
-            for zz in range(4):
-                for yy in range(4):
-                    n = base + axis_part(p, side, 1, yy) + axis_part(p, side, 2, zz)
-                    lo = (zz * 4 + yy) * ROWS
-                    put(n, res[lo:lo + ROWS])
+            for m, zz in enumerate(zs):
+                for n, yy in enumerate(ys):
+                    r = (m * len(ys) + n) * ROWS
+                    put(base + axis_part(p, side, 1, yy) + axis_part(p, side, 2, zz), res[r:r + ROWS])
             return carry
 
-        lax.fori_loop(0, 4, step, 0)
+        lax.fori_loop(0, 2 if p == 1 else 4, step, 0, unroll=UNROLL)
 
     def half_copy(p, h, n):
         b = lax.div(n, 32)
@@ -362,21 +371,29 @@
         lax.fori_loop(0, GROUP, step, 0)
         rs_copy(p, i).start()
 
-    for p in range(PIECES):
-        def put_out(n, val):
+    def put_out(p):
+        def put(n, val):
             sib_out[p, n, :, :USED[p]] = val.astype(BF16)
-        down(t, p, put_out)
+        return put
+
+    def put_total(p):
+        def put(n, val):
+            total[p, n, :, :USED[p]] = val
+        return put
+
+    for p in range(PIECES):
+        down(t, p, 1 - bit5(p, t), put_out(p))
         half_copy(p, 0, theirs[p]).start()
     for p in range(PIECES):
-        half_copy(p, 1, theirs[p]).start()
-    for p in range(PIECES):
-        def put_total(n, val):
-            total[p, n, :, :USED[p]] = val
-        down(s, p, put_total)
+        down(s, p, 1 - bit5(p, s), put_total(p))
         half_copy(p, 0, own[p]).wait_recv()
         for i in (3, 2, 1, 0):
             give(p, i)
     for p in range(PIECES):
+        down(t, p, bit5(p, t), put_out(p))
+        half_copy(p, 1, theirs[p]).start()
+    for p in range(PIECES):
+        down(s, p, bit5(p, s), put_total(p))
         half_copy(p, 1, own[p]).wait_recv()
     for i, before in ((5, (3,)), (4, (2,)), (6, (1, 5))):
         for p in range(PIECES):
@@ -422,16 +439,6 @@
     closed = a2a(pack2, got2, b2b_send, b2b_recv)
     for copy in closed:
         copy.wait()
-    row = lax.broadcasted_iota(jnp.int32, (8, 16), 0)
-    col = lax.broadcasted_iota(jnp.int32, (8, 16), 1)
-    for j in range(4):
-        for c in range(4):
-            hit = (row < 4) & (col == c * 4 + row)
-            value = jnp.dot(jnp.where(hit, 1.0, 0.0).astype(BF16), got2[j], preferred_element_type=F32)
-            w = 512 if c < 3 else 256
-            lo = QUARTER * j + 512 * c
-            moe_out[:, lo:lo + w] = value[:4, :w].astype(BF16)
-
     for mask in range(1, 8):
         cube_copy(mask).wait_send()
         back_copy(mask).wait_send()
@@ -448,15 +455,28 @@
         pltpu.make_async_copy(att.at[r], att_out.at[r], att_sem.at[r]).wait()
 
 
+def finish(got, att, moe_out, att_out):
+    att_out[...] = att[...]
+    row = lax.broadcasted_iota(jnp.int32, (8, 16), 0)
+    col = lax.broadcasted_iota(jnp.int32, (8, 16), 1)
+    for j in range(4):
+        for c in range(4):
+            hit = (row < 4) & (col == c * 4 + row)
+            value = jnp.dot(jnp.where(hit, 1.0, 0.0).astype(BF16), got[j], preferred_element_type=F32)
+            w = 512 if c < 3 else 256
+            lo = QUARTER * j + 512 * c
+            moe_out[:, lo:lo + w] = value[:4, :w].astype(BF16)
+
+
 def per_device(tokens, routes, gates, w_gate, w_up, w_down, queries, cache, lengths):
     vmem = pl.BlockSpec(memory_space=pltpu.VMEM)
     smem = pl.BlockSpec(memory_space=pltpu.SMEM)
     hbm = pl.BlockSpec(memory_space=pl.ANY)
     dma = pltpu.SemaphoreType.DMA
-    return pl.pallas_call(
+    got, att = pl.pallas_call(
         kernel,
         out_shape=(
-            jax.ShapeDtypeStruct((REQ, D), BF16),
+            jax.ShapeDtypeStruct((4, 16, 512), BF16),
             jax.ShapeDtypeStruct((REQ, HEADS, LATENT), BF16),
         ),
         in_specs=[vmem, vmem, vmem, smem, hbm, hbm, hbm, hbm, hbm],
@@ -470,14 +490,13 @@
             pltpu.VMEM((REQ, KEY, HEADS), BF16),
             pltpu.VMEM((REQ, HEADS, LATENT), BF16),
             pltpu.VMEM((2, 16, ROWS, 2 * UNITS), F32),
-            pltpu.VMEM((2, 256, UNITS), BF16),
-            pltpu.VMEM((2, 256, 128), F32),
+            pltpu.VMEM((2, 16, ROWS, UNITS), BF16),
+            pltpu.VMEM((2, 16, ROWS, 128), F32),
             pltpu.VMEM((PIECES, BLOCKS, ROWS, WIDTH), F32),
             pltpu.VMEM((PIECES, BLOCKS, ROWS, WIDTH), BF16),
             pltpu.VMEM((PIECES, BLOCKS, ROWS, WIDTH), BF16),
             pltpu.VMEM((PIECES, len(RETURN), GROUP, ROWS, WIDTH), BF16),
             pltpu.VMEM((PIECES, len(RETURN), GROUP, ROWS, WIDTH), BF16),
-            pltpu.VMEM((4, 16, 512), BF16),
             pltpu.VMEM((4, 16, 512), BF16),
             pltpu.VMEM((4, 16, 512), BF16),
             pltpu.VMEM((4, 16, 512), BF16),
@@ -495,6 +514,15 @@
             collective_id=0, has_side_effects=True, vmem_limit_bytes=60 * 1024 * 1024),
     )(tokens, routes, gates, lengths, w_gate, w_up, w_down,
       queries.transpose(0, 2, 1), cache.transpose(0, 2, 1))
+    return pl.pallas_call(
+        finish,
+        out_shape=(
+            jax.ShapeDtypeStruct((REQ, D), BF16),
+            jax.ShapeDtypeStruct((REQ, HEADS, LATENT), BF16),
+        ),
+        in_specs=[vmem, vmem],
+        out_specs=(vmem, vmem),
+    )(got, att)
 
 
 def solution(mesh):

time: 80.4 us -> 72.1 us (0.90); the launches traced: 80.2 us -> 71 us
  Pallas kernels: 76.2 us -> 70.4 us
  local copies, waits for them, and re-layouts: 3.33 us -> 0 us
    pallas_call x1 -> x2, Pallas kernels: 76.2 us -> 70.4 us  [the longest x1 68.4 us: per_device(): pl.pallas_call(kernel, out_shape=(jax.ShapeDtypeStruct((4, 16, 512), BF16...]
    unnamed x2 -> x0, local copies, waits for them, and re-layouts: 3.33 us -> none
where the time goes in v4:
time: 72.1 us; the launch traced here: 71 us
  Pallas kernels  70.4 us (98%)
    pallas_call x1, Pallas kernels, per_device(): pl.pallas_call(kernel, out_shape=(jax.ShapeDtypeStruct((4, 16, 512), BF16...  68.4 us
    pallas_call x1, Pallas kernels, per_device(): pl.pallas_call(finish, out_shape=(jax.ShapeDtypeStruct((REQ, D), BF16), j...  2 us

profile of v4, /device:TPU:0, one launch (start us, length us, event | category | flops | bytes accessed | tf_op | source)
XLA Modules:
  0.0 71.0 jit_solution(2173224560879010895)
XLA Ops:
  0.6 68.4 %shard_map.104 = (bf16[4,16,512]{2,1,0:T(8,128)(2,1)}, bf16[4,128,512]{2,1,0:T(8,128)(2,1)}) custom-call(bf16[4,7168]{1,0:T(4,128)(2,1)} %tokens.1, s32[4,8]{1,0:T(4,128)} %routes.1, f32[4,8]{1,0:T(4,128)} %gates.1, s32[4]{0:T(128)} %lengths.1, bf16[1,7168,256]{2,1,0:T(8,128)(2,1)} %w_gate.1, bf16[1,7168,256]{2,1,0:T(8,128)(2,1)} %w_up.1, ...), custom_call_target="tpu_custom_call" | custom-call | tf_op jit(solution)/shard_map/pallas_call | solution.py:476
  69.0 2.0 %shard_map.105 = (bf16[4,7168]{1,0:T(4,128)(2,1)}, bf16[4,128,512]{2,1,0:T(8,128)(2,1)}) custom-call(bf16[4,16,512]{2,1,0:T(8,128)(2,1)} %get-tuple-element.4.got, bf16[4,128,512]{2,1,0:T(8,128)(2,1)} %get-tuple-element.5.att), custom_call_target="tpu_custom_call" | custom-call | tf_op jit(solution)/shard_map/pallas_call | solution.py:517

commit v5 on v4

--- a/solution.py
+++ b/solution.py
@@ -17,6 +17,7 @@
 
 QUARTER = 1792
 PIECES = 3
+NEAR_FIRST = ((2, 0), (1, 0), (3, 0), (2, 1), (1, 1), (3, 1), (0, 1))
 UNROLL = True
 WIDTH = 640
 USED = (640, 640, 512)
@@ -34,10 +35,6 @@
 RETURN = ((5, 4), (5, 5), (5, 6), (5, 7), (4, 2), (4, 3), (3, 1))
 
 
-def beta_of(p, k, s):
-    return s if k < 3 else 1 - s
-
-
 def bit_of(c, beta):
     if isinstance(c, int):
         high, low = c // 2, ((c + 1) // 2) % 2
@@ -50,12 +47,10 @@
     return beta * (3 - c) + (1 - beta) * (c + 1 - 2 * lax.rem(c, 2))
 
 
-def axis_part(p, s, a, c):
-    return bit_of(c, s) * (1 << a) + bit_of(c, 1 - s) * (GROUP << ((a - p) % 3))
-
-
-def block_of(p, s, x, y, z):
-    return axis_part(p, s, 0, x) + axis_part(p, s, 1, y) + axis_part(p, s, 2, z)
+def row_part(p, s, yy, ww):
+    high = (bit_of(ww, 0) * (1 << (0 - p) % 3) + bit_of(yy, 1 - s) * (1 << (1 - p) % 3)
+            + bit_of(ww, 1) * (1 << (2 - p) % 3))
+    return 4 * bit_of(yy, s) + GROUP * high
 
 
 def flip_bits(n, mask):
@@ -70,26 +65,28 @@
     tokens, routes, gates, lengths, w_gate, w_up, w_down, queries, cache,
     got2, att_out,
     x_buf, wg, wu, wd, kv, qs, att, acc, hid, gexp, total, sib_out, sib_in, out_buf, in_buf,
-    pack, got, pack2, cube, cube_out, cube_in,
-    local_sem, att_sem, a2a_send, a2a_recv, cube_send, cube_recv, ag_send, ag_recv, sib_send, sib_recv,
-    rsib_send, rsib_recv, rs_send, rs_recv, back_send, back_recv, b2b_send, b2b_recv,
+    pack, got, cube, cube_out, cube_in,
+    local_sem, att_sem, cube_send, cube_recv, ag_send, ag_recv, sib_send, sib_recv,
+    rsib_send, rsib_recv, rs_send, rs_recv, back_send, back_recv,
 ):
     s = lax.axis_index("side")
     dev = lax.axis_index("dev")
     x, y, z = lax.rem(dev, 4), lax.rem(lax.div(dev, 4), 4), lax.div(dev, 16)
-    coords = (x, y, z)
     t = 1 - s
-
-    def chip(cx, cy, cz):
-        return cz * 16 + cy * 4 + cx
-
-    def moved(mask, beta):
-        return (s, chip(*[flip_of(c, beta) if mask >> a & 1 else c for a, c in enumerate(coords)]))
+    r, w_at = (1 - s) * x + s * z, (1 - s) * z + s * x
+
+    def chip(cr, cy, cw):
+        return (s, (1 - s) * (cw * 16 + cy * 4 + cr) + s * (cr * 16 + cy * 4 + cw))
+
+    def cube_peer(d, f):
+        return chip(lax.rem(r + d, 4), flip_of(y, s) if f else y, w_at)
 
     def partner(p, k):
-        return moved(1 << ((k + p) % 3), 1 - s)
-
-    peers = [(s, chip(lax.rem(x + d, 4), y, z)) for d in (1, 2, 3)]
+        a = (k + p) % 3
+        if a == 1:
+            return chip(r, flip_of(y, 1 - s), w_at)
+        return chip(r, y, flip_of(w_at, 0 if a == 0 else 1))
+
     sibling = (t, dev)
 
     loads = [
@@ -101,9 +98,8 @@
     ]
 
     barrier = pltpu.get_barrier_semaphore()
-    greet = [(s, chip(lax.rem(x + 2, 4), y, z)), sibling]
-    greet += [moved(mask, s) for mask in range(1, 8)]
-    greet += [moved(1 << a, 1 - s) for a in range(3)]
+    greet = [sibling] + [cube_peer(d, f) for f in (0, 1) for d in range(4) if d or f]
+    greet += [partner(p, 3) for p in range(PIECES)]
     for who in greet:
         pl.semaphore_signal(barrier, inc=1, device_id=who, device_id_type=MESH)
     for load in loads:
@@ -130,53 +126,45 @@
 
     pl.semaphore_wait(barrier, len(greet))
 
-    def a2a(src, dst, send, recv):
-        copies = []
-        for i, who in enumerate(peers):
-            to = lax.rem(x + i + 1, 4)
-            copies.append(pltpu.make_async_remote_copy(
-                src_ref=src.at[to], dst_ref=dst.at[x], send_sem=send.at[i], recv_sem=recv.at[i],
-                device_id=who, device_id_type=MESH))
-        for copy in copies:
-            copy.start()
-        dst[x] = src[x]
-        return copies
-
-    opened = a2a(pack, got, a2a_send, a2a_recv)
-    for copy in opened:
-        copy.wait()
-    rows = got[...].reshape(64, 512)
-    row = lax.broadcasted_iota(jnp.int32, (16, 64), 0)
-    col = lax.broadcasted_iota(jnp.int32, (16, 64), 1)
-    assembled = []
-    for c in range(4):
-        select = jnp.where(col == (row >> 2) * 16 + c * 4 + (row & 3), 1.0, 0.0).astype(BF16)
-        assembled.append(jnp.dot(select, rows, preferred_element_type=F32).astype(BF16))
-    assembled = jnp.concatenate(assembled, 1)
-
-    own = [block_of(p, s, x, y, z) for p in range(PIECES)]
-    theirs = [block_of(p, t, x, y, z) for p in range(PIECES)]
+    own = [r + row_part(p, s, y, w_at) for p in range(PIECES)]
+    theirs = [w_at + row_part(p, t, y, r) for p in range(PIECES)]
     low = lax.rem(own[0], GROUP)
     high = [lax.div(n, GROUP) for n in own]
     high_theirs = [lax.div(n, GROUP) for n in theirs]
-    cube[low] = assembled[:, :PIECES * WIDTH]
-
-    def cube_copy(mask):
-        return pltpu.make_async_remote_copy(
-            src_ref=cube.at[low], dst_ref=cube.at[low],
-            send_sem=cube_send.at[mask - 1], recv_sem=cube_recv.at[mask - 1],
-            device_id=moved(mask, s), device_id_type=MESH)
-
-    def cube_arrival(mask):
-        came = cube.at[flip_bits(low, mask)]
-        return pltpu.make_async_remote_copy(
-            src_ref=came, dst_ref=came,
-            send_sem=cube_send.at[mask - 1], recv_sem=cube_recv.at[mask - 1],
-            device_id=moved(mask, s), device_id_type=MESH)
+
+    def place_of(d, f):
+        mine = lax.div(low, 4)
+        return lax.rem(r + d, 4) + 4 * (1 - mine if f else mine)
+
+    def cube_copy(d, f):
+        return pltpu.make_async_remote_copy(
+            src_ref=pack, dst_ref=got.at[low],
+            send_sem=cube_send.at[d + 4 * f], recv_sem=cube_recv.at[d + 4 * f],
+            device_id=cube_peer(d, f), device_id_type=MESH)
+
+    def cube_arrival(d, f):
+        return pltpu.make_async_remote_copy(
+            src_ref=pack, dst_ref=got.at[place_of(4 - d, f)],
+            send_sem=cube_send.at[d + 4 * f], recv_sem=cube_recv.at[d + 4 * f],
+            device_id=cube_peer(d, f), device_id_type=MESH)
 
     def half_start(h):
         mine = lax.div(low, 4)
         return 4 * (mine if h == 0 else 1 - mine)
+
+    row = lax.broadcasted_iota(jnp.int32, (64, 64), 0)
+    col = lax.broadcasted_iota(jnp.int32, (64, 64), 1)
+    swap = ((row >> 4) == ((col >> 2) & 3)) & (((row >> 2) & 3) == (col >> 4)) & ((row & 3) == (col & 3))
+    swap = jnp.where(swap, 1.0, 0.0).astype(BF16)
+
+    def assemble(h):
+        begin = half_start(h)
+        for j in range(4):
+            rows = got[pl.ds(begin, 4), j].reshape(64, 512)
+            turned = jnp.dot(swap, rows, preferred_element_type=F32).astype(BF16)
+            for c in range(4):
+                wide = 512 if c < 3 else 384
+                cube[begin + j, :, 512 * c:512 * c + wide] = turned[16 * c:16 * (c + 1), :wide]
 
     def ag_copy(p, i):
         k, unit, h = PLAN[i]
@@ -216,20 +204,23 @@
         pltpu.make_async_copy(att.at[r], att_out.at[r], att_sem.at[r]).start()
 
     acc[...] = jnp.zeros_like(acc)
-    for mask in (3, 1, 2, 7, 5, 6, 4):
-        cube_copy(mask).start()
+    for d, f in NEAR_FIRST:
+        cube_copy(d, f).start()
+    got[low] = pack[...]
     loads[0].wait()
     loads[1].wait()
     attend(0)
     attend(1)
-    for mask in (1, 2, 3):
-        cube_arrival(mask).wait_recv()
+    for d in (1, 3, 2):
+        cube_arrival(d, 0).wait_recv()
+    assemble(0)
     for i in (0, 2, 4):
         for p in range(PIECES):
             ag_copy(p, i).start()
     attend(2)
-    for mask in (4, 5, 6, 7):
-        cube_arrival(mask).wait_recv()
+    for d in (0, 1, 3, 2):
+        cube_arrival(d, 1).wait_recv()
+    assemble(1)
     for i in (1, 3, 9):
         for p in range(PIECES):
             ag_copy(p, i).start()
@@ -246,22 +237,22 @@
                 ag_copy(p, i).start()
             forward(p, unit, high[p], s).start()
 
-    def two_of(side, b):
+    def half_rows(side, p, b):
+        every = (0, 1, 2, 3)
+        if p == 0:
+            return (2 * b, 2 * b + 1), every
+        if p == 1:
+            return (b, 3 - b), every
         beta = 1 - side
-        return (beta * 2 * b + (1 - beta) * b, beta * (2 * b + 1) + (1 - beta) * (3 - b))
+        return every, (beta * 2 * b + (1 - beta) * b, beta * (2 * b + 1) + (1 - beta) * (3 - b))
 
     def project(side, p, b):
         w = USED[p]
-        every = (0, 1, 2, 3)
-        pair = two_of(side, b)
-        zs = pair if p == 0 else every
-        ys = pair if p == 2 else every
-
-        def step(i, carry):
-            q = pair[0] + i * (pair[1] - pair[0]) if p == 1 else i
-            base = axis_part(p, side, 0, q)
+        zs, ys = half_rows(side, p, b)
+
+        def step(q, carry):
             tiles = [
-                x_buf[side, p, base + axis_part(p, side, 1, yy) + axis_part(p, side, 2, zz), :, :w]
+                x_buf[side, p, q + row_part(p, side, yy, zz), :, :w]
                 for zz in zs for yy in ys]
             lhs = jnp.concatenate(tiles, 0)
             deep = pl.ds(pl.multiple_of(q * QUARTER + p * WIDTH, 128), w)
@@ -269,14 +260,17 @@
                 res = jnp.dot(lhs, weight[deep, :], preferred_element_type=F32)
                 for m, zz in enumerate(zs):
                     for n, yy in enumerate(ys):
-                        r = (m * len(ys) + n) * ROWS
-                        acc[side, zz * 4 + yy, :, lo:lo + UNITS] += res[r:r + ROWS]
+                        at = (m * len(ys) + n) * ROWS
+                        acc[side, zz * 4 + yy, :, lo:lo + UNITS] += res[at:at + ROWS]
             return carry
 
-        lax.fori_loop(0, 2 if p == 1 else 4, step, 0, unroll=UNROLL)
+        lax.fori_loop(0, 4, step, 0, unroll=UNROLL)
 
     def bit5(p, side):
-        return bit_of(coords[(5 + p) % 3], 1 - side)
+        if p == 2:
+            return bit_of(y, 1 - side)
+        other = (1 - side) * z + side * x
+        return bit_of(other, 1 - p)
 
     loads[2].wait()
     loads[3].wait()
@@ -306,7 +300,7 @@
         gate, upper = both[:, :UNITS], both[:, UNITS:]
         hid[side] = (gate / (1.0 + jnp.exp(-gate)) * upper).astype(BF16).reshape(16, ROWS, UNITS)
         tiles = [
-            x_buf[side, 2, axis_part(2, side, 1, yy) + axis_part(2, side, 2, zz), :, 512:640]
+            x_buf[side, 2, row_part(2, side, yy, zz), :, 512:640]
             for zz in range(4) for yy in range(4)]
         gexp[side] = jnp.dot(
             jnp.concatenate(tiles, 0), select, preferred_element_type=F32).reshape(16, ROWS, 128)
@@ -314,26 +308,21 @@
 
     def down(side, p, b, put):
         w = USED[p]
-        every = (0, 1, 2, 3)
-        pair = two_of(side, b)
-        zs = pair if p == 0 else every
-        ys = pair if p == 2 else every
+        zs, ys = half_rows(side, p, b)
         lhs = jnp.concatenate([hid[side, zz * 4 + yy] for zz in zs for yy in ys], 0)
         share = jnp.concatenate([gexp[side, zz * 4 + yy] for zz in zs for yy in ys], 0)
         share = jnp.concatenate([share] * (w // 128), 1)
 
-        def step(i, carry):
-            q = pair[0] + i * (pair[1] - pair[0]) if p == 1 else i
+        def step(q, carry):
             wide = pl.ds(pl.multiple_of(q * QUARTER + p * WIDTH, 128), w)
             res = jnp.dot(lhs, wd[:, wide], preferred_element_type=F32) * share
-            base = axis_part(p, side, 0, q)
             for m, zz in enumerate(zs):
                 for n, yy in enumerate(ys):
-                    r = (m * len(ys) + n) * ROWS
-                    put(base + axis_part(p, side, 1, yy) + axis_part(p, side, 2, zz), res[r:r + ROWS])
+                    at = (m * len(ys) + n) * ROWS
+                    put(q + row_part(p, side, yy, zz), res[at:at + ROWS])
             return carry
 
-        lax.fori_loop(0, 2 if p == 1 else 4, step, 0, unroll=UNROLL)
+        lax.fori_loop(0, 4, step, 0, unroll=UNROLL)
 
     def half_copy(p, h, n):
         b = lax.div(n, 32)
@@ -404,44 +393,43 @@
         for slot in (0, 4, 6):
             rs_copy(p, slot).wait_recv()
 
-    def back_copy(mask):
-        return pltpu.make_async_remote_copy(
-            src_ref=cube_out.at[flip_bits(low, mask)], dst_ref=cube_in.at[low],
-            send_sem=back_send.at[mask - 1], recv_sem=back_recv.at[mask - 1],
-            device_id=moved(mask, s), device_id_type=MESH)
-
-    def back_arrival(mask):
-        came = cube_in.at[flip_bits(low, mask)]
+    def back_copy(d, f):
+        return pltpu.make_async_remote_copy(
+            src_ref=cube_out.at[place_of(d, f)], dst_ref=cube_in.at[low],
+            send_sem=back_send.at[d + 4 * f], recv_sem=back_recv.at[d + 4 * f],
+            device_id=cube_peer(d, f), device_id_type=MESH)
+
+    def back_arrival(d, f):
+        came = cube_in.at[place_of(4 - d, f)]
         return pltpu.make_async_remote_copy(
             src_ref=came, dst_ref=came,
-            send_sem=back_send.at[mask - 1], recv_sem=back_recv.at[mask - 1],
-            device_id=moved(mask, s), device_id_type=MESH)
-
-    for mask in (7, 3, 5, 6, 1, 2, 4):
-        to = flip_bits(low, mask)
-        for p in range(PIECES):
-            cube_out[to, :, WIDTH * p:WIDTH * p + USED[p]] = summed(p, 0, to).astype(BF16)
-        back_copy(mask).start()
-    result = jnp.concatenate([summed(p, 0, low) for p in range(PIECES)], 1)
-    for mask in (4, 2, 1, 6, 5, 3, 7):
-        back_arrival(mask).wait_recv()
-        result += cube_in[flip_bits(low, mask)].astype(F32)
-    result = jnp.concatenate([result.astype(BF16), jnp.zeros((ROWS, 256), BF16)], 1)
-
-    row = lax.broadcasted_iota(jnp.int32, (64, 16), 0)
-    col = lax.broadcasted_iota(jnp.int32, (64, 16), 1)
-    packed = jnp.zeros((64, 512), F32)
-    for c in range(4):
-        hit = (((row >> 2) & 3) == c) & (col == (row >> 4) * 4 + (row & 3))
-        packed += jnp.dot(jnp.where(hit, 1.0, 0.0).astype(BF16), result[:, 512 * c:512 * (c + 1)],
-                          preferred_element_type=F32)
-    pack2[...] = packed.astype(BF16).reshape(4, 16, 512)
-    closed = a2a(pack2, got2, b2b_send, b2b_recv)
-    for copy in closed:
-        copy.wait()
-    for mask in range(1, 8):
-        cube_copy(mask).wait_send()
-        back_copy(mask).wait_send()
+            send_sem=back_send.at[d + 4 * f], recv_sem=back_recv.at[d + 4 * f],
+            device_id=cube_peer(d, f), device_id_type=MESH)
+
+    def part_out(h):
+        begin = half_start(h)
+        for j in range(4):
+            whole = jnp.concatenate(
+                [summed(p, 0, begin + j).astype(BF16) for p in range(PIECES)] + [jnp.zeros((ROWS, 256), BF16)], 1)
+            stacked = jnp.concatenate([whole[:, 512 * c:512 * (c + 1)] for c in range(4)], 0)
+            turned = jnp.dot(swap, stacked, preferred_element_type=F32).astype(BF16)
+            cube_out[pl.ds(begin, 4), j] = turned.reshape(4, ROWS, 512)
+
+    part_out(1)
+    for d in (2, 1, 3, 0):
+        back_copy(d, 1).start()
+    part_out(0)
+    for d in (2, 1, 3):
+        back_copy(d, 0).start()
+    result = cube_out[low].astype(F32)
+    for d, f in ((1, 0), (3, 0), (0, 1), (2, 0), (1, 1), (3, 1), (2, 1)):
+        back_arrival(d, f).wait_recv()
+        result += cube_in[place_of(4 - d, f)].astype(F32)
+    got2[...] = result.astype(BF16)
+
+    for d, f in NEAR_FIRST:
+        cube_copy(d, f).wait_send()
+        back_copy(d, f).wait_send()
     for p in range(PIECES):
         for i in range(len(PLAN)):
             ag_copy(p, i).wait_send()
@@ -498,17 +486,15 @@
             pltpu.VMEM((PIECES, len(RETURN), GROUP, ROWS, WIDTH), BF16),
             pltpu.VMEM((PIECES, len(RETURN), GROUP, ROWS, WIDTH), BF16),
             pltpu.VMEM((4, 16, 512), BF16),
-            pltpu.VMEM((4, 16, 512), BF16),
-            pltpu.VMEM((4, 16, 512), BF16),
+            pltpu.VMEM((GROUP, 4, ROWS, 512), BF16),
             pltpu.VMEM((GROUP, ROWS, PIECES * WIDTH), BF16),
-            pltpu.VMEM((GROUP, ROWS, QUARTER), BF16),
-            pltpu.VMEM((GROUP, ROWS, QUARTER), BF16),
-            dma((5,)), dma((REQ,)), dma((3,)), dma((3,)), dma((7,)), dma((7,)),
+            pltpu.VMEM((GROUP, 4, ROWS, 512), BF16),
+            pltpu.VMEM((GROUP, 4, ROWS, 512), BF16),
+            dma((5,)), dma((REQ,)), dma((8,)), dma((8,)),
             dma((PIECES, len(PLAN))), dma((PIECES, len(PLAN))),
             dma((PIECES, 8)), dma((PIECES, 8)),
             dma((PIECES, 2)), dma((PIECES, 2)),
-            dma((PIECES, len(RETURN))), dma((PIECES, len(RETURN))), dma((7,)), dma((7,)),
-            dma((3,)), dma((3,)),
+            dma((PIECES, len(RETURN))), dma((PIECES, len(RETURN))), dma((8,)), dma((8,)),
         ],
         compiler_params=pltpu.CompilerParams(
             collective_id=0, has_side_effects=True, vmem_limit_bytes=60 * 1024 * 1024),

time: 72.1 us -> 64.2 us (0.89); the launches traced: 71 us -> 64 us
  Pallas kernels: 70.4 us -> 63.4 us
    pallas_call x1, Pallas kernels: 68.4 us -> 61.4 us  [per_device(): pl.pallas_call(kernel, out_shape=(jax.ShapeDtypeStruct((4, 16, 512), BF16...]
where the time goes in v5:
time: 64.2 us; the launch traced here: 64 us
  Pallas kernels  63.4 us (99%)
    pallas_call x1, Pallas kernels, per_device(): pl.pallas_call(kernel, out_shape=(jax.ShapeDtypeStruct((4, 16, 512), BF16...  61.4 us
    pallas_call x1, Pallas kernels, per_device(): pl.pallas_call(finish, out_shape=(jax.ShapeDtypeStruct((REQ, D), BF16), j...  2 us

profile of v5, /device:TPU:0, one launch (start us, length us, event | category | flops | bytes accessed | tf_op | source)
XLA Modules:
  0.0 64.0 jit_solution(5458370001208458652)
XLA Ops:
  0.6 61.4 %shard_map.104 = (bf16[4,16,512]{2,1,0:T(8,128)(2,1)}, bf16[4,128,512]{2,1,0:T(8,128)(2,1)}) custom-call(bf16[4,7168]{1,0:T(4,128)(2,1)} %tokens.1, s32[4,8]{1,0:T(4,128)} %routes.1, f32[4,8]{1,0:T(4,128)} %gates.1, s32[4]{0:T(128)} %lengths.1, bf16[1,7168,256]{2,1,0:T(8,128)(2,1)} %w_gate.1, bf16[1,7168,256]{2,1,0:T(8,128)(2,1)} %w_up.1, ...), custom_call_target="tpu_custom_call" | custom-call | tf_op jit(solution)/shard_map/pallas_call | solution.py:464
  62.0 2.0 %shard_map.105 = (bf16[4,7168]{1,0:T(4,128)(2,1)}, bf16[4,128,512]{2,1,0:T(8,128)(2,1)}) custom-call(bf16[4,16,512]{2,1,0:T(8,128)(2,1)} %get-tuple-element.4.got, bf16[4,128,512]{2,1,0:T(8,128)(2,1)} %get-tuple-element.5.att), custom_call_target="tpu_custom_call" | custom-call | tf_op jit(solution)/shard_map/pallas_call | solution.py:503

commit v6 on v5

--- a/solution.py
+++ b/solution.py
@@ -62,9 +62,9 @@
 
 
 def kernel(
-    tokens, routes, gates, lengths, w_gate, w_up, w_down, queries, cache,
+    tokens_in, routes_in, gates_in, lengths_in, w_gate, w_up, w_down, queries, cache,
     got2, att_out,
-    x_buf, wg, wu, wd, kv, qs, att, acc, hid, gexp, total, sib_out, sib_in, out_buf, in_buf,
+    tokens, routes, gates, lengths, x_buf, wg, wu, wd, kv, qs, att, acc, hid, gexp, total, sib_out, sib_in, out_buf, in_buf,
     pack, got, cube, cube_out, cube_in,
     local_sem, att_sem, cube_send, cube_recv, ag_send, ag_recv, sib_send, sib_recv,
     rsib_send, rsib_recv, rs_send, rs_recv, back_send, back_recv,
@@ -96,14 +96,22 @@
         pltpu.make_async_copy(w_up.at[0], wu, local_sem.at[3]),
         pltpu.make_async_copy(w_down.at[0], wd, local_sem.at[4]),
     ]
+    small = [
+        pltpu.make_async_copy(tokens_in, tokens, local_sem.at[5]),
+        pltpu.make_async_copy(routes_in, routes, local_sem.at[6]),
+        pltpu.make_async_copy(gates_in, gates, local_sem.at[7]),
+        pltpu.make_async_copy(lengths_in, lengths, local_sem.at[8]),
+    ]
 
     barrier = pltpu.get_barrier_semaphore()
     greet = [sibling] + [cube_peer(d, f) for f in (0, 1) for d in range(4) if d or f]
     greet += [partner(p, 3) for p in range(PIECES)]
     for who in greet:
         pl.semaphore_signal(barrier, inc=1, device_id=who, device_id_type=MESH)
-    for load in loads:
+    for load in small + loads:
         load.start()
+    for load in small:
+        load.wait()
 
     lane = lax.broadcasted_iota(jnp.int32, (4, 128), 1)
     dense = jnp.zeros((4, 128), F32)
@@ -458,7 +466,6 @@
 
 def per_device(tokens, routes, gates, w_gate, w_up, w_down, queries, cache, lengths):
     vmem = pl.BlockSpec(memory_space=pltpu.VMEM)
-    smem = pl.BlockSpec(memory_space=pltpu.SMEM)
     hbm = pl.BlockSpec(memory_space=pl.ANY)
     dma = pltpu.SemaphoreType.DMA
     got, att = pl.pallas_call(
@@ -467,9 +474,13 @@
             jax.ShapeDtypeStruct((4, 16, 512), BF16),
             jax.ShapeDtypeStruct((REQ, HEADS, LATENT), BF16),
         ),
-        in_specs=[vmem, vmem, vmem, smem, hbm, hbm, hbm, hbm, hbm],
+        in_specs=[hbm] * 9,
         out_specs=(vmem, hbm),
         scratch_shapes=[
+            pltpu.VMEM((REQ, D), BF16),
+            pltpu.VMEM((REQ, 8), jnp.int32),
+            pltpu.VMEM((REQ, 8), F32),
+            pltpu.SMEM((REQ,), jnp.int32),
             pltpu.VMEM((2, PIECES, BLOCKS, ROWS, WIDTH), BF16),
             pltpu.VMEM((D, UNITS), BF16),
             pltpu.VMEM((D, UNITS), BF16),
@@ -490,7 +501,7 @@
             pltpu.VMEM((GROUP, ROWS, PIECES * WIDTH), BF16),
             pltpu.VMEM((GROUP, 4, ROWS, 512), BF16),
             pltpu.VMEM((GROUP, 4, ROWS, 512), BF16),
-            dma((5,)), dma((REQ,)), dma((8,)), dma((8,)),
+            dma((9,)), dma((REQ,)), dma((8,)), dma((8,)),
             dma((PIECES, len(PLAN))), dma((PIECES, len(PLAN))),
             dma((PIECES, 8)), dma((PIECES, 8)),
             dma((PIECES, 2)), dma((PIECES, 2)),

time: 64.2 us -> 63.5 us (0.989)
  no operation moved by 1% of the time
where the time goes in v6:
time: 63.5 us; the launch traced here: 63.4 us
  Pallas kernels  62.8 us (99%)
  between operations  0.64 us (1%)
    pallas_call x1, Pallas kernels, per_device(): pl.pallas_call(kernel, out_shape=(jax.ShapeDtypeStruct((4, 16, 512), BF16...  60.8 us
    pallas_call x1, Pallas kernels, per_device(): pl.pallas_call(finish, out_shape=(jax.ShapeDtypeStruct((REQ, D), BF16), j...  2 us

profile of v6, /device:TPU:0, one launch (start us, length us, event | category | flops | bytes accessed | tf_op | source)
XLA Modules:
  0.0 63.4 jit_solution(2095807866434890555)
XLA Ops:
  0.6 60.8 %shard_map.104 = (bf16[4,16,512]{2,1,0:T(8,128)(2,1)}, bf16[4,128,512]{2,1,0:T(8,128)(2,1)}) custom-call(bf16[4,7168]{1,0:T(4,128)(2,1)} %tokens_in.1, s32[4,8]{1,0:T(4,128)} %routes_in.1, f32[4,8]{1,0:T(4,128)} %gates_in.1, s32[4]{0:T(128)} %lengths_in.1, bf16[1,7168,256]{2,1,0:T(8,128)(2,1)} %w_gate.1, bf16[1,7168,256]{2,1,0:T(8,128)(2,1)} %w_up.1, ...), custom_call_target="tpu_custom_call" | custom-call | tf_op jit(solution)/shard_map/pallas_call | solution.py:471
  61.4 2.0 %shard_map.105 = (bf16[4,7168]{1,0:T(4,128)(2,1)}, bf16[4,128,512]{2,1,0:T(8,128)(2,1)}) custom-call(bf16[4,16,512]{2,1,0:T(8,128)(2,1)} %get-tuple-element.4.got, bf16[4,128,512]{2,1,0:T(8,128)(2,1)} %get-tuple-element.5.att), custom_call_target="tpu_custom_call" | custom-call | tf_op jit(solution)/shard_map/pallas_call | solution.py:514

commit v7 on v6

--- a/solution.py
+++ b/solution.py
@@ -284,11 +284,16 @@
     loads[3].wait()
     for p in range(PIECES):
         project(s, p, bit5(p, s))
+    for unit, arrived in ((4, (4, 9)),):
+        for p in range(PIECES):
+            for i in arrived:
+                ag_arrival(p, i).wait_recv()
+            forward(p, unit, high[p], s).start()
     for p in range(PIECES):
         for unit in range(4):
             forward(p, unit, high_theirs[p], t).wait_recv()
         project(t, p, bit5(p, t))
-    for unit, arrived in ((4, (4, 9)), (5, (6,)), (6, (7,)), (7, (8,))):
+    for unit, arrived in ((5, (6,)), (6, (7,)), (7, (8,)),):
         for p in range(PIECES):
             for i in arrived:
                 ag_arrival(p, i).wait_recv()

time: 63.5 us -> 62.9 us (level)
  no operation moved by 1% of the time
where the time goes in v7:
time: 62.9 us; the launch traced here: 62.8 us
  Pallas kernels  62.2 us (99%)
  between operations  0.64 us (1%)
    pallas_call x1, Pallas kernels, per_device(): pl.pallas_call(kernel, out_shape=(jax.ShapeDtypeStruct((4, 16, 512), BF16...  60.2 us
    pallas_call x1, Pallas kernels, per_device(): pl.pallas_call(finish, out_shape=(jax.ShapeDtypeStruct((REQ, D), BF16), j...  2 us

profile of v7, /device:TPU:0, one launch (start us, length us, event | category | flops | bytes accessed | tf_op | source)
XLA Modules:
  0.0 62.8 jit_solution(2292730078456401139)
XLA Ops:
  0.6 60.2 %shard_map.104 = (bf16[4,16,512]{2,1,0:T(8,128)(2,1)}, bf16[4,128,512]{2,1,0:T(8,128)(2,1)}) custom-call(bf16[4,7168]{1,0:T(4,128)(2,1)} %tokens_in.1, s32[4,8]{1,0:T(4,128)} %routes_in.1, f32[4,8]{1,0:T(4,128)} %gates_in.1, s32[4]{0:T(128)} %lengths_in.1, bf16[1,7168,256]{2,1,0:T(8,128)(2,1)} %w_gate.1, bf16[1,7168,256]{2,1,0:T(8,128)(2,1)} %w_up.1, ...), custom_call_target="tpu_custom_call" | custom-call | tf_op jit(solution)/shard_map/pallas_call | solution.py:476
  60.8 2.0 %shard_map.105 = (bf16[4,7168]{1,0:T(4,128)(2,1)}, bf16[4,128,512]{2,1,0:T(8,128)(2,1)}) custom-call(bf16[4,16,512]{2,1,0:T(8,128)(2,1)} %get-tuple-element.4.got, bf16[4,128,512]{2,1,0:T(8,128)(2,1)} %get-tuple-element.5.att), custom_call_target="tpu_custom_call" | custom-call | tf_op jit(solution)/shard_map/pallas_call | solution.py:519
